TPU v7x, 128 devices: a whole 4x4x4 slice. The times are simulated.
128 devices in a mesh: ctx: 32 (over y_lo, z, x), head: 4 (over y_hi, core).
Axes of the slice: x: 4, y: 4 (y_hi: 2, y_lo: 2; y = y_hi * 2 + y_lo), z: 4, core: 2. Of those that a mesh axis runs over, the one named last changes fastest.
Arguments:
- query_raw: bfloat16 [32768, 4096], P('ctx', 'head')
- key_raw: bfloat16 [32768, 1024], P('ctx', 'head')
- values: bfloat16 [32768, 1024], P('ctx', 'head'), may hold values from -6 to 6
- output_gradient: bfloat16 [32768, 4096], P('ctx', 'head'), may hold values from -6 to 6
- query_gain: float32 [4096], P('head'), may hold values from 0.5 to 3
- key_norm_gain: float32 [1024], P('head'), may hold values from 0.5 to 3
- block_docs: int32 [256], replicated, may hold values from 0 to 41, never falling along the last dimension, each value on 1 to 24 neighbouring positions
Outputs:
- attended: bfloat16 [32768, 4096], P('ctx', 'head')
- query_grad: bfloat16 [32768, 4096], P('ctx', 'head')
- key_raw_gradient: bfloat16 [32768, 1024], P('ctx', 'head')
- value_grad: bfloat16 [32768, 1024], P('ctx', 'head')
- query_gain_grad: float32 [4096], P('head')
- key_gain_grad: float32 [1024], P('head')
Inputs may be any that keep to these rules, and one draw needn't show every extreme that they name: `block_docs`: document numbers never fall from one block to the next; each document covers 1 to 24 consecutive mask blocks, and one covers exactly 24.
All inputs are finite; a program needn't handle non-finite values.
Results may differ from a plain program's by a relative error of at most 0.024.
The roundings to bfloat16 on the way count: a program that leaves them out, or rounds other values in their place, can miss the bound.
Values may be sent and summed in bfloat16 or wider, within the bound.
A program may use at most 128 MiB of HBM per device.

v0:
```python
import jax
import jax.numpy as jnp
from jax import lax
from jax.sharding import PartitionSpec as P

QUERY_HEADS = 32
KEY_VALUE_HEADS = 8
HEAD_SIZE = 128
WINDOW_REACH = 512
BLOCK = 128


EPS = 1e-06
NEGATIVE = -1e30


def from_behind(array, axis, by):
    peers = lax.axis_size(axis)
    pairs = [(i, i + by) for i in range(peers) if 0 <= i + by < peers]
    return lax.ppermute(array, axis, pairs)


def rescale_each_row(floats, summed, gain, row_width):
    scale_rows = lax.rsqrt(summed / row_width + EPS)[:, None]
    unit_rows = floats * scale_rows
    return (scale_rows, unit_rows, (unit_rows * gain).astype(jnp.bfloat16))


def send_back(key_gradient_total, value_gradient_total, halo_rows):
    return from_behind(
        (
            key_gradient_total[halo_rows - WINDOW_REACH : halo_rows],
            value_gradient_total[halo_rows - WINDOW_REACH : halo_rows],
        ),
        "ctx",
        -1,
    )


def local(query_raw, key_raw, values, output_gradient, query_gain, key_norm_gain, block_docs):
    tok_rows = query_raw.shape[0]
    query_cols = query_raw.shape[1]
    key_cols = key_raw.shape[1]
    kv_heads = key_cols // HEAD_SIZE
    query_group_count = query_cols // key_cols
    stride_rows = min(512, WINDOW_REACH)
    softmax_scale = HEAD_SIZE ** (-0.5)
    query_float = query_raw.astype(jnp.float32)
    key_single_precision = key_raw.astype(jnp.float32)
    query_sq, key_squared = lax.psum(
        (
            jnp.sum(query_float * query_float, axis=1),
            jnp.sum(key_single_precision * key_single_precision, axis=1),
        ),
        "head",
    )
    query_scale, query_unit, query_normalized = rescale_each_row(
        query_float, query_sq, query_gain, QUERY_HEADS * HEAD_SIZE
    )
    key_inverse_scale, key_unit_rows, key_normalized = rescale_each_row(
        key_single_precision, key_squared, key_norm_gain, KEY_VALUE_HEADS * HEAD_SIZE
    )
    halo_keys, halo_values = from_behind((key_normalized, values), "ctx", 1)
    halo_rows = halo_keys.shape[0]
    ext_keys = jnp.concatenate([halo_keys, key_normalized])
    ext_values = jnp.concatenate([halo_values, values])
    first_block = lax.axis_index("ctx") * (tok_rows // BLOCK)
    doc_padded = jnp.concatenate([jnp.full((halo_rows // BLOCK,), -1, jnp.int32), block_docs])
    doc_ext = jnp.repeat(
        lax.dynamic_slice_in_dim(doc_padded, first_block, (halo_rows + tok_rows) // BLOCK, 0), BLOCK
    )
    doc_query = doc_ext[halo_rows:]
    key_total_count = stride_rows + WINDOW_REACH
    distance = (
        jnp.arange(stride_rows, dtype=jnp.int32)[:, None]
        + WINDOW_REACH
        - jnp.arange(key_total_count, dtype=jnp.int32)[None, :]
    )
    in_window = (distance >= 0) & (distance < WINDOW_REACH)

    def attend(running, block_index):
        key_gradient_total, value_gradient_total = running
        leading_row = block_index * stride_rows
        lowest = halo_rows - WINDOW_REACH + leading_row
        query_block = lax.dynamic_slice_in_dim(
            query_normalized, leading_row, stride_rows, 0
        ).reshape(stride_rows, kv_heads, query_group_count, HEAD_SIZE)
        gradient_block = lax.dynamic_slice_in_dim(
            output_gradient, leading_row, stride_rows, 0
        ).reshape(stride_rows, kv_heads, query_group_count, HEAD_SIZE)
        key_block = lax.dynamic_slice_in_dim(ext_keys, lowest, key_total_count, 0).reshape(
            key_total_count, kv_heads, HEAD_SIZE
        )
        value_block = lax.dynamic_slice_in_dim(ext_values, lowest, key_total_count, 0).reshape(
            key_total_count, kv_heads, HEAD_SIZE
        )
        doc_rows = lax.dynamic_slice_in_dim(doc_query, leading_row, stride_rows, 0)
        doc_keys = lax.dynamic_slice_in_dim(doc_ext, lowest, key_total_count, 0)
        visible = in_window & (doc_rows[:, None] == doc_keys[None, :])
        scores = (
            jnp.einsum("ighd,jgd->ghij", query_block, key_block, preferred_element_type=jnp.float32)
            * softmax_scale
        )
        row_max = jnp.max(jnp.where(visible, scores, NEGATIVE), axis=-1, keepdims=True)
        expo = jnp.where(visible, jnp.exp(scores - row_max), 0.0)
        weights = expo / jnp.sum(expo, axis=-1, keepdims=True)
        weights_low = weights.astype(jnp.bfloat16)
        out_blk = jnp.einsum(
            "ghij,jgd->ighd", weights_low, value_block, preferred_element_type=jnp.float32
        ).astype(jnp.bfloat16)
        delta = jnp.einsum(
            "ighd,ighd->ghi", gradient_block, out_blk, preferred_element_type=jnp.float32
        )
        dweights = jnp.einsum(
            "ighd,jgd->ghij", gradient_block, value_block, preferred_element_type=jnp.float32
        )
        dscores_low = (weights * (dweights - delta[..., None])).astype(jnp.bfloat16)
        dquery_blk = (
            jnp.einsum("ghij,jgd->ighd", dscores_low, key_block, preferred_element_type=jnp.float32)
            * softmax_scale
        )
        key_gradient_block = (
            jnp.einsum(
                "ghij,ighd->jgd", dscores_low, query_block, preferred_element_type=jnp.float32
            )
            * softmax_scale
        )
        value_gradient_block = jnp.einsum(
            "ghij,ighd->jgd", weights_low, gradient_block, preferred_element_type=jnp.float32
        )
        present_key = lax.dynamic_slice_in_dim(key_gradient_total, lowest, key_total_count, 0)
        key_gradient_total = lax.dynamic_update_slice_in_dim(
            key_gradient_total,
            present_key + key_gradient_block.reshape(key_total_count, key_cols),
            lowest,
            0,
        )
        present_value = lax.dynamic_slice_in_dim(value_gradient_total, lowest, key_total_count, 0)
        value_gradient_total = lax.dynamic_update_slice_in_dim(
            value_gradient_total,
            present_value + value_gradient_block.reshape(key_total_count, key_cols),
            lowest,
            0,
        )
        return (
            (key_gradient_total, value_gradient_total),
            (out_blk.reshape(stride_rows, query_cols), dquery_blk.reshape(stride_rows, query_cols)),
        )

    blank_start = jnp.zeros((halo_rows + tok_rows, key_cols), jnp.float32)
    total_blocks = tok_rows // stride_rows
    (key_gradient_total, value_gradient_total), (out_blocks, dquery_blocks) = lax.scan(
        attend, (blank_start, blank_start), jnp.arange(total_blocks, dtype=jnp.int32)
    )
    back_key, back_value = send_back(key_gradient_total, value_gradient_total, halo_rows)
    attended = out_blocks.reshape(tok_rows, query_cols)
    dquery = dquery_blocks.reshape(tok_rows, query_cols)
    tail_start = tok_rows - WINDOW_REACH
    dkey_local = key_gradient_total[halo_rows:]
    dvalue_local = value_gradient_total[halo_rows:]
    dkey = jnp.concatenate([dkey_local[:tail_start], dkey_local[tail_start:] + back_key])
    value_grad = jnp.concatenate(
        [dvalue_local[:tail_start], dvalue_local[tail_start:] + back_value]
    ).astype(jnp.bfloat16)
    query_scaled = dquery * query_gain
    key_rescaled = dkey * key_norm_gain
    query_dot, key_product = lax.psum(
        (jnp.sum(query_scaled * query_unit, axis=1), jnp.sum(key_rescaled * key_unit_rows, axis=1)),
        "head",
    )
    query_grad = (
        query_scale * (query_scaled - query_unit * (query_dot / (QUERY_HEADS * HEAD_SIZE))[:, None])
    ).astype(jnp.bfloat16)
    key_raw_gradient = (
        key_inverse_scale
        * (key_rescaled - key_unit_rows * (key_product / (KEY_VALUE_HEADS * HEAD_SIZE))[:, None])
    ).astype(jnp.bfloat16)
    query_gain_grad, key_gain_grad = lax.psum(
        (jnp.sum(dquery * query_unit, axis=0), jnp.sum(dkey * key_unit_rows, axis=0)), "ctx"
    )
    return (attended, query_grad, key_raw_gradient, value_grad, query_gain_grad, key_gain_grad)


def solution(mesh):
    placed = (
        P("ctx", "head"),
        P("ctx", "head"),
        P("ctx", "head"),
        P("ctx", "head"),
        P("head"),
        P("head"),
        P(),
    )
    return jax.shard_map(
        local,
        mesh=mesh,
        in_specs=placed,
        out_specs=(
            P("ctx", "head"),
            P("ctx", "head"),
            P("ctx", "head"),
            P("ctx", "head"),
            P("head"),
            P("head"),
        ),
        check_vma=False,
    )
```

profile of v0, /device:TPU:24, one launch (start us, length us, event | category | flops | bytes accessed | tf_op | source)
XLA Modules:
  0.0 323.4 jit_solution(7992543844339828626)
XLA Ops:
  4.1 8.3 %all-reduce.3 = (f32[1024]{0:T(1024)S(1)}, f32[1024]{0:T(1024)S(1)}) all-reduce(f32[1024]{0:T(1024)S(1)} %fusion.33, f32[1024]{0:T(1024)S(1)} %fusion.44), channel_id=1, replica_groups=mesh['ctx'=32,'head'=4] {'head'}, use_global_device_ids=true, to_apply=%region_1.0 | all-reduce | flops 2048 | bytes 16384 | tf_op jit(solution)/shard_map/psum | solution.py:50
  13.7 3.4 %collective-permute-start = (bf16[1024,256]{1,0:T(8,128)(2,1)S(1)}, bf16[1024,256]{1,0:T(8,128)(2,1)}, u32[]{:S(2)}, u32[]{:S(2)}) collective-permute-start(bf16[1024,256]{1,0:T(8,128)(2,1)S(1)} %fusion.38), channel_id=1, source_target_pairs={{0,4},{4,8},{8,12},{12,16},{16,20},{20,24},{24,28},{28,32},{32,36}... | collective-permute-start | bytes 1572872 | tf_op jit(solution)/shard_map/ppermute | solution.py:20
  18.4 3.4 %collective-permute-start.1 = (bf16[1024,256]{0,1:T(8,128)(2,1)S(1)}, bf16[1024,256]{0,1:T(8,128)(2,1)}, u32[]{:S(2)}, u32[]{:S(2)}) collective-permute-start(bf16[1024,256]{0,1:T(8,128)(2,1)S(1)} %copy.37), channel_id=1, source_target_pairs={{0,4},{4,8},{8,12},{12,16},{16,20},{20,24},{24,28},{28,32},{32,36}... | collective-permute-start | bytes 1572872 | tf_op jit(solution)/shard_map/ppermute | solution.py:20
  24.0 10.7 %collective-permute-done = bf16[1024,256]{1,0:T(8,128)(2,1)} collective-permute-done((bf16[1024,256]{1,0:T(8,128)(2,1)S(1)}, bf16[1024,256]{1,0:T(8,128)(2,1)}, u32[]{:S(2)}, u32[]{:S(2)}) %collective-permute-start) | collective-permute-done | bytes 524320 | tf_op jit(solution)/shard_map/ppermute | solution.py:20
  36.9 7.5 %collective-permute-done.1 = bf16[1024,256]{0,1:T(8,128)(2,1)} collective-permute-done((bf16[1024,256]{0,1:T(8,128)(2,1)S(1)}, bf16[1024,256]{0,1:T(8,128)(2,1)}, u32[]{:S(2)}, u32[]{:S(2)}) %collective-permute-start.1) | collective-permute-done | bytes 524320 | tf_op jit(solution)/shard_map/ppermute | solution.py:20
  49.4 154.1 %while.19 = (s32[]{:T(128)}, f32[2048,256]{1,0:T(8,128)}, f32[2048,256]{1,0:T(8,128)}, bf16[2,512,1024]{2,1,0:T(8,128)(2,1)}, f32[2,512,1024]{2,1,0:T(8,128)}, /...) while((s32[]{:T(128)}, f32[2048,256]{1,0:T(8,128)}, ...), condition=%wide.region_7.8_spmd.clone, body=%wide.region_4.7_spmd.clone.sunk | while | flops 7573599232 | bytes 245469712 | solution.py:152
  64.4 11.9 %fusion.98 = (f32[2,4,512]{2,1,0:T(4,128)S(1)}, f32[2,4,512,1024]{2,3,1,0:T(8,128)}) fusion(pred[512,1024]{0,1:T(8,128)(4,1)} %fusion.97, bf16[1024,2,128,1]{0,2,3,1:T(8,128)(2,1)S(1)} %bitcast.155, bf16[512,2,4,128]{0,3,2,1:T(8,128)(2,1)} %bitcast.152), kind=kOutput, calls=%fused_computation.84.clone.1 | convolution fusion | flops 2172650496 | bytes 18890752 | tf_op jit(solution)/shard_map/while/body/eval_jaxpr/sub | solution.py:105
  76.3 6.8 %fusion.99 = bf16[2,4,512,1024]{2,3,1,0:T(8,128)(2,1)S(1)} fusion(f32[2,4,512,1024]{2,3,1,0:T(8,128)} %get-tuple-element.347, f32[2,4,512]{2,1,0:T(4,128)S(1)} %get-tuple-element.348), kind=kLoop, calls=%fused_computation.15.clone.1 | loop fusion | flops 8388608 | bytes 25182208 | tf_op jit(solution)/shard_map/while/body/eval_jaxpr/convert_element_type | solution.py:107
  93.7 5.9 %fusion.101 = (f32[2,4,512]{2,1,0:T(4,128)S(1)}, bf16[2,128,4,512]{3,1,2,0:T(8,128)(2,1)}) fusion(bf16[512,1024]{0,1:T(8,128)(2,1)S(1)} %copy.102, bf16[1024,2,128,1]{0,2,3,1:T(8,128)(2,1)S(1)} %bitcast.157, bf16[2,4,512,1024]{2,3,1,0:T(8,128)(2,1)} %copy-done), kind=kOutput, calls=%fused_computation.17.clone.1 | convolution fusion | flops 1076359168 | bytes 11026432 | tf_op jit(solution)/shard_map/while/body/eval_jaxpr/ghij,jgd->ighd/dot_general | solution.py:108
  99.6 7.4 %fusion.102 = bf16[2,4,512,1024]{2,3,1,0:T(8,128)(2,1)S(1)} fusion(f32[2,4,512]{2,1,0:T(4,128)S(1)} %get-tuple-element.349, f32[2,4,512,1024]{2,3,1,0:T(8,128)} %get-tuple-element.347, f32[2,4,512]{2,1,0:T(4,128)S(1)} %get-tuple-element.348, bf16[1024,2,128,1]{0,2,3,1:T(8,128)(2,1)} %bitcast.158, bf16[512,2,4,128]{0,3,2,1:T(8,128)(2,1)S(1)} %bitcast.150), kind=kOutput, calls=%fused_computation.4.clone.1 | convolution fusion | flops 1090519040 | bytes 26771456 | tf_op jit(solution)/shard_map/while/body/eval_jaxpr/ighd,jgd->ghij/dot_general | solution.py:114
  107.0 2.8 fusion.103
  117.0 6.1 %convolution_multiply_fusion.2 = f32[2,128,4,512]{3,1,2,0:T(8,128)} fusion(bf16[1024,2,128,1]{0,2,3,1:T(8,128)(2,1)S(1)} %bitcast.156, bf16[2,4,512,1024]{2,3,1,0:T(8,128)(2,1)} %copy-done.1), kind=kOutput, calls=%fused_computation.23.clone.1 | convolution fusion | flops 1074266112 | bytes 11010048 | tf_op jit(solution)/shard_map/while/body/eval_jaxpr/ghij,jgd->ighd/dot_general | solution.py:119
  141.5 11.9 %fusion.98 = (f32[2,4,512]{2,1,0:T(4,128)S(1)}, f32[2,4,512,1024]{2,3,1,0:T(8,128)}) fusion(pred[512,1024]{0,1:T(8,128)(4,1)} %fusion.97, bf16[1024,2,128,1]{0,2,3,1:T(8,128)(2,1)S(1)} %bitcast.155, bf16[512,2,4,128]{0,3,2,1:T(8,128)(2,1)} %bitcast.152), kind=kOutput, calls=%fused_computation.84.clone.1 | convolution fusion | flops 2172650496 | bytes 18890752 | tf_op jit(solution)/shard_map/while/body/eval_jaxpr/sub | solution.py:105
  153.4 6.8 %fusion.99 = bf16[2,4,512,1024]{2,3,1,0:T(8,128)(2,1)S(1)} fusion(f32[2,4,512,1024]{2,3,1,0:T(8,128)} %get-tuple-element.347, f32[2,4,512]{2,1,0:T(4,128)S(1)} %get-tuple-element.348), kind=kLoop, calls=%fused_computation.15.clone.1 | loop fusion | flops 8388608 | bytes 25182208 | tf_op jit(solution)/shard_map/while/body/eval_jaxpr/convert_element_type | solution.py:107
  170.8 5.9 %fusion.101 = (f32[2,4,512]{2,1,0:T(4,128)S(1)}, bf16[2,128,4,512]{3,1,2,0:T(8,128)(2,1)}) fusion(bf16[512,1024]{0,1:T(8,128)(2,1)S(1)} %copy.102, bf16[1024,2,128,1]{0,2,3,1:T(8,128)(2,1)S(1)} %bitcast.157, bf16[2,4,512,1024]{2,3,1,0:T(8,128)(2,1)} %copy-done), kind=kOutput, calls=%fused_computation.17.clone.1 | convolution fusion | flops 1076359168 | bytes 11026432 | tf_op jit(solution)/shard_map/while/body/eval_jaxpr/ghij,jgd->ighd/dot_general | solution.py:108
  176.7 7.4 %fusion.102 = bf16[2,4,512,1024]{2,3,1,0:T(8,128)(2,1)S(1)} fusion(f32[2,4,512]{2,1,0:T(4,128)S(1)} %get-tuple-element.349, f32[2,4,512,1024]{2,3,1,0:T(8,128)} %get-tuple-element.347, f32[2,4,512]{2,1,0:T(4,128)S(1)} %get-tuple-element.348, bf16[1024,2,128,1]{0,2,3,1:T(8,128)(2,1)} %bitcast.158, bf16[512,2,4,128]{0,3,2,1:T(8,128)(2,1)S(1)} %bitcast.150), kind=kOutput, calls=%fused_computation.4.clone.1 | convolution fusion | flops 1090519040 | bytes 26771456 | tf_op jit(solution)/shard_map/while/body/eval_jaxpr/ighd,jgd->ghij/dot_general | solution.py:114
  184.1 2.8 fusion.103
  194.1 6.1 %convolution_multiply_fusion.2 = f32[2,128,4,512]{3,1,2,0:T(8,128)} fusion(bf16[1024,2,128,1]{0,2,3,1:T(8,128)(2,1)S(1)} %bitcast.156, bf16[2,4,512,1024]{2,3,1,0:T(8,128)(2,1)} %copy-done.1), kind=kOutput, calls=%fused_computation.23.clone.1 | convolution fusion | flops 1074266112 | bytes 11010048 | tf_op jit(solution)/shard_map/while/body/eval_jaxpr/ghij,jgd->ighd/dot_general | solution.py:119
  204.6 3.8 %collective-permute-start.2 = (f32[512,256]{1,0:T(8,128)S(1)}, f32[512,256]{1,0:T(8,128)S(1)}, u32[]{:S(2)}, u32[]{:S(2)}) collective-permute-start(f32[512,256]{1,0:T(8,128)S(1)} %slice.36), channel_id=1, source_target_pairs={{4,0},{8,4},{12,8},{16,12},{20,16},{24,20},{28,24},{32,28},{36,32}... | collective-permute-start | bytes 1572872 | tf_op jit(solution)/shard_map/ppermute | solution.py:20
  214.2 4.0 %fusion.32 = (f32[1024]{0:T(1024)S(1)}, f32[1024]{0:T(1024)S(1)}) fusion(bf16[1024,1024]{1,0:T(8,128)(2,1)} %param.9, f32[2,512,1024]{2,1,0:T(8,128)} %get-tuple-element.171, f32[1024]{0:T(1024)S(1)} %copy-done.15, f32[1024]{0:T(1024)S(1)} %copy-done.17), kind=kLoop, calls=%fused_computation.53 | loop fusion | flops 7337984 | bytes 6307840 | tf_op jit(solution)/shard_map/reduce_sum | solution.py:179
  218.2 3.3 %collective-permute-done.2 = f32[512,256]{1,0:T(8,128)S(1)} collective-permute-done((f32[512,256]{1,0:T(8,128)S(1)}, f32[512,256]{1,0:T(8,128)S(1)}, u32[]{:S(2)}, u32[]{:S(2)}) %collective-permute-start.2) | collective-permute-done | bytes 524320 | tf_op jit(solution)/shard_map/ppermute | solution.py:20
  223.0 7.3 %all-reduce.2 = (f32[1024]{0:T(1024)S(1)}, f32[1024]{0:T(1024)S(1)}) all-reduce(f32[1024]{0:T(1024)S(1)} %get-tuple-element.217, f32[1024]{0:T(1024)S(1)} %get-tuple-element.219), channel_id=1, replica_groups=mesh['ctx'=32,'head'=4] {'head'}, use_global_device_ids=true, to_apply=%region_9.10 | all-reduce | flops 2048 | bytes 16384 | tf_op jit(solution)/shard_map/psum | solution.py:167
  232.5 4.4 %fusion.31 = bf16[1024,1024]{1,0:T(8,128)(2,1)} fusion(bf16[1024,1024]{1,0:T(8,128)(2,1)S(1)} %copy-done.9, f32[2,512,1024]{2,1,0:T(8,128)} %get-tuple-element.171, f32[1024]{0:T(1024)S(1)} %get-tuple-element.261, f32[1024]{0:T(1024)S(1)} %copy-done.17, f32[1024]{0:T(1024)S(1)} %copy-done.15), kind=kLoop, calls=%fused_computation.52 | loop fusion | flops 7340032 | bytes 8400896 | tf_op jit(solution)/shard_map/convert_element_type | solution.py:173
  239.0 84.4 %all-reduce.1 = (f32[1024]{0:T(1024)}, f32[256]{0:T(256)}) all-reduce(f32[1024]{0:T(1024)S(1)} %get-tuple-element.216, f32[256]{0:T(256)S(1)} %get-tuple-element.218), channel_id=1, replica_groups=mesh['ctx'=32,'head'=4] {'ctx'}, use_global_device_ids=true, to_apply=%region_13.14 | all-reduce | flops 1280 | bytes 10240 | tf_op jit(solution)/shard_map/psum | solution.py:178
  (134 shorter events, 98.8 us)
Async XLA Ops:
  0.6 21.4 %copy-start.8 = (bf16[1024,1024]{1,0:T(8,128)(2,1)S(1)}, bf16[1024,1024]{1,0:T(8,128)(2,1)}, u32[]{:S(2)}) copy-start(bf16[1024,1024]{1,0:T(8,128)(2,1)} %param.9) | copy-start | bytes 6291460
  0.6 21.2 %copy-start.19 = (s32[256]{0:T(256)S(1)}, s32[256]{0:T(256)}, u32[]{:S(2)}) copy-start(s32[256]{0:T(256)} %param.15) | copy-start | bytes 3076
  0.7 21.3 %copy-start.16 = (f32[1024]{0:T(1024)S(1)}, f32[1024]{0:T(1024)}, u32[]{:S(2)}) copy-start(f32[1024]{0:T(1024)} %param.13) | copy-start | bytes 12292
  13.7 21.1 %collective-permute-start = (bf16[1024,256]{1,0:T(8,128)(2,1)S(1)}, bf16[1024,256]{1,0:T(8,128)(2,1)}, u32[]{:S(2)}, u32[]{:S(2)}) collective-permute-start(bf16[1024,256]{1,0:T(8,128)(2,1)S(1)} %fusion.38), channel_id=1, source_target_pairs={{0,4},{4,8},{8,12},{12,16},{16,20},{20,24},{24,28},{28,32},{32,36}... | collective-permute-start | bytes 1572872 | tf_op jit(solution)/shard_map/ppermute | solution.py:20
  18.4 26.0 %collective-permute-start.1 = (bf16[1024,256]{0,1:T(8,128)(2,1)S(1)}, bf16[1024,256]{0,1:T(8,128)(2,1)}, u32[]{:S(2)}, u32[]{:S(2)}) collective-permute-start(bf16[1024,256]{0,1:T(8,128)(2,1)S(1)} %copy.37), channel_id=1, source_target_pairs={{0,4},{4,8},{8,12},{12,16},{16,20},{20,24},{24,28},{28,32},{32,36}... | collective-permute-start | bytes 1572872 | tf_op jit(solution)/shard_map/ppermute | solution.py:20
  49.4 164.7 %copy-start.15 = (f32[1024]{0:T(1024)S(1)}, f32[1024]{0:T(1024)}, u32[]{:S(2)}) copy-start(f32[1024]{0:T(1024)} %copy-done.14) | copy-start | bytes 12292
  49.4 164.8 %copy-start.17 = (f32[1024]{0:T(1024)S(1)}, f32[1024]{0:T(1024)}, u32[]{:S(2)}) copy-start(f32[1024]{0:T(1024)} %param.13) | copy-start | bytes 12292
  59.8 4.6 %copy-start.5 = (bf16[1024,256]{0,1:T(8,128)(2,1)S(1)}, bf16[1024,256]{0,1:T(8,128)(2,1)}, u32[]{:S(2)}) copy-start(bf16[1024,256]{0,1:T(8,128)(2,1)} %copy.103) | copy-start | bytes 1572868 | tf_op jit(solution)/shard_map/while
  83.1 3.2 copy-start
  93.7 5.9 %copy-start.6 = (bf16[1024,256]{0,1:T(8,128)(2,1)}, bf16[1024,256]{0,1:T(8,128)(2,1)S(1)}, u32[]{:S(2)}) copy-start(bf16[1024,256]{0,1:T(8,128)(2,1)S(1)} %constant_dynamic-slice_fusion.17) | copy-start | bytes 1572868 | tf_op jit(solution)/shard_map/while
  99.6 7.4 %copy-start.2 = (bf16[512,1024]{0,1:T(8,128)(2,1)S(1)}, bf16[512,1024]{0,1:T(8,128)(2,1)}, u32[]{:S(2)}) copy-start(bf16[512,1024]{0,1:T(8,128)(2,1)} %copy.104) | copy-start | bytes 3145732 | tf_op jit(solution)/shard_map/while
  107.0 3.2 copy-start.1
  136.9 4.6 %copy-start.5 = (bf16[1024,256]{0,1:T(8,128)(2,1)S(1)}, bf16[1024,256]{0,1:T(8,128)(2,1)}, u32[]{:S(2)}) copy-start(bf16[1024,256]{0,1:T(8,128)(2,1)} %copy.103) | copy-start | bytes 1572868 | tf_op jit(solution)/shard_map/while
  160.2 3.2 copy-start
  170.8 5.9 %copy-start.6 = (bf16[1024,256]{0,1:T(8,128)(2,1)}, bf16[1024,256]{0,1:T(8,128)(2,1)S(1)}, u32[]{:S(2)}) copy-start(bf16[1024,256]{0,1:T(8,128)(2,1)S(1)} %constant_dynamic-slice_fusion.17) | copy-start | bytes 1572868 | tf_op jit(solution)/shard_map/while
  176.7 7.4 %copy-start.2 = (bf16[512,1024]{0,1:T(8,128)(2,1)S(1)}, bf16[512,1024]{0,1:T(8,128)(2,1)}, u32[]{:S(2)}) copy-start(bf16[512,1024]{0,1:T(8,128)(2,1)} %copy.104) | copy-start | bytes 3145732 | tf_op jit(solution)/shard_map/while
  184.1 3.2 copy-start.1
  204.6 16.9 %copy-start.7 = (f32[2048,256]{1,0:T(8,128)S(1)}, f32[2048,256]{1,0:T(8,128)}, u32[]{:S(2)}) copy-start(f32[2048,256]{1,0:T(8,128)} %get-tuple-element.172) | copy-start | bytes 6291460
  204.6 16.9 %collective-permute-start.2 = (f32[512,256]{1,0:T(8,128)S(1)}, f32[512,256]{1,0:T(8,128)S(1)}, u32[]{:S(2)}, u32[]{:S(2)}) collective-permute-start(f32[512,256]{1,0:T(8,128)S(1)} %slice.36), channel_id=1, source_target_pairs={{4,0},{8,4},{12,8},{16,12},{20,16},{24,20},{28,24},{32,28},{36,32}... | collective-permute-start | bytes 1572872 | tf_op jit(solution)/shard_map/ppermute | solution.py:20
  211.4 25.5 %collective-permute-start.3 = (f32[512,256]{1,0:T(8,128)}, f32[512,256]{1,0:T(8,128)}, u32[]{:S(2)}, u32[]{:S(2)}) collective-permute-start(f32[512,256]{1,0:T(8,128)} %slice.39), channel_id=1, source_target_pairs={{4,0},{8,4},{12,8},{16,12},{20,16},{24,20},{28,24},{32,28},{36,32}... | collective-permute-start | bytes 1572872 | tf_op jit(solution)/shard_map/ppermute | solution.py:20
  214.2 8.2 %copy-start.10 = (bf16[1024,256]{1,0:T(8,128)(2,1)S(1)}, bf16[1024,256]{1,0:T(8,128)(2,1)}, u32[]{:S(2)}) copy-start(bf16[1024,256]{1,0:T(8,128)(2,1)} %param.10) | copy-start | bytes 1572868
  214.2 8.2 %copy-start.13 = (f32[1024]{0:T(1024)S(1)}, f32[1024]{0:T(1024)}, u32[]{:S(2)}) copy-start(f32[1024]{0:T(1024)} %copy-done.12) | copy-start | bytes 12292
  214.2 8.2 %copy-start.18 = (f32[256]{0:T(256)S(1)}, f32[256]{0:T(256)}, u32[]{:S(2)}) copy-start(f32[256]{0:T(256)} %param.14) | copy-start | bytes 3076
  218.2 14.2 %copy-start.9 = (bf16[1024,1024]{1,0:T(8,128)(2,1)S(1)}, bf16[1024,1024]{1,0:T(8,128)(2,1)}, u32[]{:S(2)}) copy-start(bf16[1024,1024]{1,0:T(8,128)(2,1)} %param.9) | copy-start | bytes 6291460
  (7 other events, 16.2 us)
where the time goes:
time: 325 us; the launch traced here: 323 us
  blocking collectives  100 us (31%)
  matrix products  73.6 us (23%)
  local copies, waits for them, and re-layouts  67.1 us (21%)
  other arithmetic  45.4 us (14%)
  waiting for transfers between devices  21.5 us (7%)
  starting transfers between devices  13.3 us (4%)
    psum x1, blocking collectives, local(): lax.psum((jnp.sum(dquery * query_unit, axis=0), jnp.sum(dkey * key_unit_r...  84.4 us
    sub x2, matrix products, attend(): expo = jnp.where(visible, jnp.exp(scores - row_max), 0.0)  23.7 us
    ppermute x4, waiting for transfers between devices, from_behind(): return lax.ppermute(array, axis, pairs)  21.5 us
    dot_general x2, matrix products, attend(): jnp.einsum('ighd,jgd->ghij', gradient_block, value_block, preferred_eleme...  14.8 us
    convert_element_type x2, other arithmetic, attend(): weights_low = weights.astype(jnp.bfloat16)  13.6 us
    ppermute x4, starting transfers between devices, from_behind(): return lax.ppermute(array, axis, pairs)  13.3 us
    dot_general x2, matrix products, attend(): jnp.einsum('ghij,jgd->ighd', dscores_low, key_block, preferred_element_ty...  12.2 us
    dynamic_update_slice x8, local copies, waits for them, and re-layouts, local(): lax.scan(attend, (blank_start, blank_start), jnp.arange(total_blocks, dty...  11.9 us
  transfers between devices with their start and end apart: 4, of which 3 were waited for; matrix products, arithmetic and copies ran while one was open for 6% of the time, Pallas kernels for 0%

commit v1 on v0

v1 whole, which is shorter than its diff:
```python
import jax
import jax.numpy as jnp
from jax import lax
from jax.experimental import pallas as pl
from jax.experimental.pallas import tpu as pltpu
from jax.sharding import PartitionSpec as P

QUERY_HEADS = 32
KEY_VALUE_HEADS = 8
HEAD_SIZE = 128
WINDOW_REACH = 512
BLOCK = 128
EPS = 1e-06
NEGATIVE = -1e30
SCALE = HEAD_SIZE ** (-0.5)
SCALE_LOG2 = SCALE * 1.4426950408889634

F32 = jnp.float32
BF16 = jnp.bfloat16
MESH = pl.DeviceIdType.MESH

TOKENS = 1024
BLOCKS_HERE = TOKENS // BLOCK
HALO = WINDOW_REACH
HALO_BLOCKS = HALO // BLOCK
WINDOW_BLOCKS = HALO_BLOCKS + 1
WINDOW = WINDOW_BLOCKS * BLOCK
EXT = HALO + TOKENS
GROUPS = 2
GROUP = 4
HEADS = GROUPS * GROUP
QCOLS = HEADS * HEAD_SIZE
KCOLS = GROUPS * HEAD_SIZE
HEAD_PEERS = 4
GAIN_ROWS = 16


def dot(a, b, ca, cb):
    return lax.dot_general(a, b, (((ca,), (cb,)), ((), ())), preferred_element_type=F32)


def block_rows(b):
    return pl.ds(pl.multiple_of(b * BLOCK, BLOCK), BLOCK)


def cols(t):
    return slice(t * 128, (t + 1) * 128)


def column(row):
    return jnp.broadcast_to(row, (128, 128)).T


def row_sums(tile):
    return jnp.sum(tile.T, axis=0, keepdims=True)


def eight(tile):
    return jnp.sum(tile.reshape(16, 8, tile.shape[1]), axis=0)


def kernel(
    q_in, k_in, v_in, g_in, q_gain, k_gain, docs,
    att_out, qg_out, kg_out, vg_out, qgain_out, kgain_out,
    q_raw, go, att, qgrad, u_all, qn,
    k_raw, vals, kn, k_t, v_t, dk, dv,
    back_k, back_v, got_k, got_v, kgrad, vgrad,
    q_col, k_col, tri,
    stat, stat_all, k_stat, halo_stat,
    inner, inner_all, kin, kin_all, hin, hin_all, hin_sum, hin_got,
    q_acc, k_acc, gains, gains_x, gains_z, gains_y,
    load_sem, out_sem, halo_send, halo_recv, stat_send, stat_recv,
    inner_send, inner_recv, back_send, back_recv, kin_send, kin_recv,
    hin_send, hin_recv, gain_send, gain_recv,
):
    ctx = lax.axis_index("ctx")
    head = lax.axis_index("head")
    x = ctx % 4
    z = (ctx // 4) % 4
    y = ctx // 16
    nxt = (ctx + 1) % 32
    prv = (ctx + 31) % 32

    def at_x(r):
        return (y * 4 + z) * 4 + (x + r) % 4

    def at_z(r):
        return (y * 4 + (z + r) % 4) * 4 + x

    at_y = (((y + 1) % 2) * 4 + z) * 4 + x

    def at_head(r):
        return (head + r) % HEAD_PEERS

    def remote(src, dst, send, recv, **where):
        return pltpu.make_async_remote_copy(
            src_ref=src, dst_ref=dst, send_sem=send, recv_sem=recv,
            device_id=where, device_id_type=MESH,
        )

    barrier = pltpu.get_barrier_semaphore()
    for r in range(1, 4):
        pl.semaphore_signal(barrier, inc=1, device_id={"head": at_head(r)}, device_id_type=MESH)
        pl.semaphore_signal(barrier, inc=1, device_id={"ctx": at_x(r)}, device_id_type=MESH)
        pl.semaphore_signal(barrier, inc=1, device_id={"ctx": at_z(r)}, device_id_type=MESH)
    for other in (nxt, prv, at_y):
        pl.semaphore_signal(barrier, inc=1, device_id={"ctx": other}, device_id_type=MESH)

    own = pl.ds(HALO, TOKENS)
    load_k = pltpu.make_async_copy(k_in, k_raw.at[own], load_sem.at[0])
    load_q = pltpu.make_async_copy(q_in, q_raw, load_sem.at[1])
    load_v = pltpu.make_async_copy(v_in, vals.at[own], load_sem.at[2])
    load_g = pltpu.make_async_copy(g_in, go, load_sem.at[3])
    load_k.start()
    load_q.start()
    load_v.start()
    load_g.start()

    pl.semaphore_wait(barrier, 12)
    tail = pl.ds(TOKENS - HALO, HALO)
    front = pl.ds(0, HALO)
    halo_copies = [
        remote(k_in.at[tail], k_raw.at[front], halo_send.at[0], halo_recv.at[0], ctx=nxt),
        remote(v_in.at[tail], vals.at[front], halo_send.at[1], halo_recv.at[1], ctx=nxt),
    ]
    for copy in halo_copies:
        copy.start()

    load_k.wait()
    load_q.wait()

    def squares(b, _):
        rows = block_rows(b)
        total = None
        for t in range(HEADS):
            part = q_raw[rows, cols(t)].astype(F32)
            total = part * part if total is None else total + part * part
        stat[pl.ds(b, 1), :] = row_sums(total)
        total = None
        for t in range(GROUPS):
            part = k_raw[block_rows(b + HALO_BLOCKS), cols(t)].astype(F32)
            total = part * part if total is None else total + part * part
        stat[pl.ds(b + 8, 1), :] = row_sums(total)
        return 0

    lax.fori_loop(0, BLOCKS_HERE, squares, 0)
    stat_copies = [
        remote(stat, stat_all.at[head], stat_send.at[r - 1], stat_recv.at[r - 1], head=at_head(r))
        for r in range(1, 4)
    ]
    for copy in stat_copies:
        copy.start()
    stat_all[head] = stat[...]

    key_at = lax.broadcasted_iota(jnp.int32, (BLOCK, BLOCK), 0)
    query_at = lax.broadcasted_iota(jnp.int32, (BLOCK, BLOCK), 1)
    tri[0] = jnp.where(key_at > query_at, 0.0, NEGATIVE)
    tri[1] = jnp.where(key_at <= query_at, 0.0, NEGATIVE)
    dk[...] = jnp.zeros_like(dk)
    dv[...] = jnp.zeros_like(dv)
    q_acc[...] = jnp.zeros_like(q_acc)
    k_acc[...] = jnp.zeros_like(k_acc)
    load_v.wait()

    def turn_values(b, _):
        rows = block_rows(b)
        for t in range(GROUPS):
            v_t[cols(t), rows] = vals[rows, cols(t)].T
        return 0

    lax.fori_loop(HALO_BLOCKS, EXT // BLOCK, turn_values, 0)

    for copy in stat_copies:
        copy.wait_recv()
    total = stat_all[0] + stat_all[1] + stat_all[2] + stat_all[3]
    k_stat[...] = total[8:16]
    relay = remote(k_stat, halo_stat, halo_send.at[2], halo_recv.at[2], ctx=nxt)
    relay.start()

    q_scale = lax.rsqrt(total[0:8] / (QUERY_HEADS * HEAD_SIZE) + EPS)
    for b in range(BLOCKS_HERE):
        q_col[b * BLOCK : (b + 1) * BLOCK] = column(q_scale[b : b + 1])

    def norm_keys(b, scale_row):
        rows = slice(b * BLOCK, (b + 1) * BLOCK)
        scale = column(scale_row)
        k_col[rows] = scale
        for t in range(GROUPS):
            unit = k_raw[rows, cols(t)].astype(F32) * scale
            normed = (unit * k_gain[:, cols(t)]).astype(BF16)
            kn[rows, cols(t)] = normed
            k_t[cols(t), rows] = normed.T

    k_scale = lax.rsqrt(total[8:16] / (KEY_VALUE_HEADS * HEAD_SIZE) + EPS)
    for b in range(BLOCKS_HERE):
        norm_keys(b + HALO_BLOCKS, k_scale[b : b + 1])
    load_g.wait()

    def order(s):
        return jnp.where(s < 3, s + 4, jnp.where(s < 7, s - 3, 7))

    def att_copy(b):
        rows = block_rows(b)
        return pltpu.make_async_copy(att.at[rows], att_out.at[rows], out_sem.at[0, b])

    def qgrad_copy(b):
        rows = block_rows(b)
        return pltpu.make_async_copy(qgrad.at[rows], qg_out.at[rows], out_sem.at[1, b])

    def inner_copies(b):
        return [
            remote(
                inner.at[b], inner_all.at[head, b],
                inner_send.at[r - 1, b], inner_recv.at[r - 1, b], head=at_head(r),
            )
            for r in range(1, 4)
        ]

    def finish_queries(b):
        rows = block_rows(b)
        for copy in inner_copies(b):
            copy.wait_recv()
        summed = inner_all[0, b] + inner_all[1, b] + inner_all[2, b] + inner_all[3, b]
        mean = column(summed[0:1] / (QUERY_HEADS * HEAD_SIZE))
        scale = q_col[rows]
        for t in range(HEADS):
            unit = q_raw[rows, cols(t)].astype(F32) * scale
            qgrad[rows, cols(t)] = (scale * (u_all[rows, cols(t)] - unit * mean)).astype(BF16)
        qgrad_copy(b).start()

    def attend(b, biases, g):
        rows = block_rows(b)
        window = pl.ds(pl.multiple_of(b * BLOCK, BLOCK), WINDOW)
        gc = cols(g)
        queries = jnp.concatenate([qn[:, cols(g * GROUP + h)] for h in range(GROUP)], axis=0)
        grads = jnp.concatenate([go[rows, cols(g * GROUP + h)] for h in range(GROUP)], axis=0)
        scores = dot(kn[window, gc], queries, 1, 1)
        first = jnp.concatenate([tri[0]] * GROUP, axis=1)
        last = jnp.concatenate([tri[1]] * GROUP, axis=1)
        parts = [scores[c * BLOCK : (c + 1) * BLOCK] for c in range(WINDOW_BLOCKS)]
        parts[0] = parts[0] + first
        parts[-1] = parts[-1] + last
        top = None
        for part, bias in zip(parts, biases):
            here = jnp.max(part, axis=0, keepdims=True) + bias
            top = here if top is None else jnp.maximum(top, here)
        top = top * SCALE_LOG2
        expo = [
            jnp.exp2(part * SCALE_LOG2 - (top - bias)) for part, bias in zip(parts, biases)
        ]
        inverse = 1.0 / sum(jnp.sum(e, axis=0, keepdims=True) for e in expo)
        weights = jnp.concatenate([e * inverse for e in expo], axis=0)
        weights_low = weights.astype(BF16)
        dweights = dot(vals[window, gc], grads, 1, 1)
        delta = jnp.sum(weights * dweights, axis=0, keepdims=True)
        dscores_low = (weights * (dweights - delta)).astype(BF16)
        out_t = dot(v_t[gc, window], weights_low, 1, 0)
        dquery_t = dot(k_t[gc, window], dscores_low, 1, 0)
        dv[window, gc] += dot(weights_low, grads, 1, 0)
        dk[window, gc] += dot(dscores_low, queries, 1, 0)
        scale = q_col[rows]
        product = None
        for h in range(GROUP):
            hc = cols(g * GROUP + h)
            att[rows, hc] = out_t[:, cols(h)].T.astype(BF16)
            dquery = dquery_t[:, cols(h)].T * SCALE
            onto = dquery * (q_raw[rows, hc].astype(F32) * scale)
            q_acc[:, hc] += eight(onto)
            gain = q_gain[:, hc]
            u_all[rows, hc] = dquery * gain
            product = onto * gain if product is None else product + onto * gain
        return product

    def back_copies(b):
        rows = block_rows(b)
        return [
            remote(back_k.at[rows], got_k.at[rows], back_send.at[0, b], back_recv.at[0, b], ctx=prv),
            remote(back_v.at[rows], got_v.at[rows], back_send.at[1, b], back_recv.at[1, b], ctx=prv),
        ]

    def send_back(b):
        rows = block_rows(b)
        scale = k_col[rows]
        product = None
        for t in range(GROUPS):
            dkey = dk[rows, cols(t)] * SCALE
            onto = dkey * (k_raw[rows, cols(t)].astype(F32) * scale)
            k_acc[:, cols(t)] += eight(onto)
            back_k[rows, cols(t)] = dkey.astype(BF16)
            back_v[rows, cols(t)] = dv[rows, cols(t)].astype(BF16)
            gain = k_gain[:, cols(t)]
            product = onto * gain if product is None else product + onto * gain
        for copy in back_copies(b):
            copy.start()
        hin[pl.ds(b, 1), :] = row_sums(product)

    def exchange(src, dst, send, recv):
        return [
            remote(src, dst.at[head], send.at[r - 1], recv.at[r - 1], head=at_head(r))
            for r in range(1, 4)
        ]

    hin_copies = exchange(hin, hin_all, hin_send, hin_recv)

    def step(s, _):
        b = order(s)
        rows = block_rows(b)

        @pl.when(s == 3)
        def _():
            for copy in halo_copies:
                copy.wait_recv()
            relay.wait_recv()
            halo_scale = lax.rsqrt(halo_stat[...] / (KEY_VALUE_HEADS * HEAD_SIZE) + EPS)
            for n in range(HALO_BLOCKS):
                norm_keys(n, halo_scale[n + HALO_BLOCKS : n + HALO_BLOCKS + 1])
            lax.fori_loop(0, HALO_BLOCKS, turn_values, 0)

        here = ctx * BLOCKS_HERE + b
        doc = docs[here]
        biases = []
        for c in range(WINDOW_BLOCKS):
            there = here - HALO_BLOCKS + c
            same = (docs[jnp.maximum(there, 0)] == doc) & (there >= 0)
            biases.append(jnp.where(same, 0.0, NEGATIVE))

        scale = q_col[rows]
        for t in range(HEADS):
            unit = q_raw[rows, cols(t)].astype(F32) * scale
            qn[:, cols(t)] = (unit * q_gain[:, cols(t)]).astype(BF16)

        product = attend(b, biases, 0) + attend(b, biases, 1)
        att_copy(b).start()
        tile = jnp.broadcast_to(row_sums(product), (8, 128))
        inner[b] = tile
        inner_all[head, b] = tile
        for copy in inner_copies(b):
            copy.start()

        @pl.when((s >= 3) & (s < 7))
        def _():
            send_back(s - 3)

        @pl.when(s == 6)
        def _():
            hin_all[head] = hin[...]
            for copy in hin_copies:
                copy.start()

        @pl.when((s >= 1) & (s < 7))
        def _():
            finish_queries(order(s - 1))

        return 0

    hin[...] = jnp.zeros_like(hin)
    lax.fori_loop(0, BLOCKS_HERE, step, 0)

    def own_keys(b, _):
        rows = block_rows(b + HALO_BLOCKS)
        scale = k_col[rows]
        product = None
        for t in range(GROUPS):
            onto = dk[rows, cols(t)] * SCALE * (k_raw[rows, cols(t)].astype(F32) * scale)
            k_acc[:, cols(t)] += eight(onto)
            gain = k_gain[:, cols(t)]
            product = onto * gain if product is None else product + onto * gain
        kin[pl.ds(b, 1), :] = row_sums(product)
        return 0

    lax.fori_loop(0, BLOCKS_HERE, own_keys, 0)
    for t in range(HEADS):
        gains[t : t + 1] = jnp.sum(q_acc[:, cols(t)], axis=0, keepdims=True)
    for t in range(GROUPS):
        gains[HEADS + t : HEADS + t + 1] = jnp.sum(k_acc[:, cols(t)], axis=0, keepdims=True)
    gains[HEADS + GROUPS :] = jnp.zeros((GAIN_ROWS - HEADS - GROUPS, 128), F32)
    x_copies = [
        remote(gains, gains_x.at[x], gain_send.at[r - 1], gain_recv.at[r - 1], ctx=at_x(r))
        for r in range(1, 4)
    ]
    for copy in x_copies:
        copy.start()
    gains_x[x] = gains[...]
    kin_copies = exchange(kin, kin_all, kin_send, kin_recv)
    for copy in kin_copies:
        copy.start()
    kin_all[head] = kin[...]

    for copy in hin_copies:
        copy.wait_recv()
    hin_sum[...] = hin_all[0] + hin_all[1] + hin_all[2] + hin_all[3]
    hin_back = remote(hin_sum, hin_got, hin_send.at[3], hin_recv.at[3], ctx=prv)
    hin_back.start()

    finish_queries(3)

    for copy in x_copies:
        copy.wait_recv()
    mine = gains_x[0] + gains_x[1] + gains_x[2] + gains_x[3]
    gains_z[z] = mine
    z_copies = [
        remote(
            gains_z.at[z], gains_z.at[z], gain_send.at[r + 2], gain_recv.at[r + 2], ctx=at_z(r)
        )
        for r in range(1, 4)
    ]
    for copy in z_copies:
        copy.start()

    finish_queries(7)

    for copy in z_copies:
        copy.wait_recv()
    gains_y[y] = gains_z[0] + gains_z[1] + gains_z[2] + gains_z[3]
    y_copy = remote(gains_y.at[y], gains_y.at[y], gain_send.at[6], gain_recv.at[6], ctx=at_y)
    y_copy.start()

    for n in range(HALO_BLOCKS):
        for copy in back_copies(n):
            copy.wait_recv()
    split = TOKENS - HALO
    vgrad[0:split] = dv[HALO : HALO + split].astype(BF16)
    vgrad[split:] = (dv[HALO + split :] + got_v[...].astype(F32)).astype(BF16)
    v_copy = pltpu.make_async_copy(vgrad, vg_out, load_sem.at[4])
    v_copy.start()

    for copy in kin_copies:
        copy.wait_recv()
    hin_back.wait_recv()
    kin_total = kin_all[0] + kin_all[1] + kin_all[2] + kin_all[3]
    got_total = hin_got[...]
    for b in range(BLOCKS_HERE):
        there = slice(b * BLOCK, (b + 1) * BLOCK)
        rows = slice(HALO + b * BLOCK, HALO + (b + 1) * BLOCK)
        row = kin_total[b : b + 1]
        n = b - (BLOCKS_HERE - HALO_BLOCKS)
        if n >= 0:
            row = row + got_total[n : n + 1]
        mean = column(row / (KEY_VALUE_HEADS * HEAD_SIZE))
        scale = k_col[rows]
        for t in range(GROUPS):
            dkey = dk[rows, cols(t)] * SCALE
            if n >= 0:
                dkey = dkey + got_k[n * BLOCK : (n + 1) * BLOCK, cols(t)].astype(F32)
            unit = k_raw[rows, cols(t)].astype(F32) * scale
            grad = scale * (dkey * k_gain[:, cols(t)] - unit * mean)
            kgrad[there, cols(t)] = grad.astype(BF16)
    k_copy = pltpu.make_async_copy(kgrad, kg_out, load_sem.at[5])
    k_copy.start()

    y_copy.wait_recv()
    summed = gains_y[0] + gains_y[1]
    for t in range(HEADS):
        qgain_out[:, cols(t)] = summed[t : t + 1]
    for t in range(GROUPS):
        kgain_out[:, cols(t)] = summed[HEADS + t : HEADS + t + 1]

    for copy in (
        halo_copies + [relay] + stat_copies + hin_copies + [hin_back] + kin_copies
        + x_copies + z_copies + [y_copy]
    ):
        copy.wait_send()
    for n in range(HALO_BLOCKS):
        for copy in back_copies(n):
            copy.wait_send()

    def drain(b, _):
        for copy in inner_copies(b):
            copy.wait_send()
        att_copy(b).wait()
        qgrad_copy(b).wait()
        return 0

    lax.fori_loop(0, BLOCKS_HERE, drain, 0)
    v_copy.wait()
    k_copy.wait()


def local(query_raw, key_raw, values, output_gradient, query_gain, key_norm_gain, block_docs):
    hbm = pl.BlockSpec(memory_space=pl.ANY)
    vmem = pl.BlockSpec(memory_space=pltpu.VMEM)
    smem = pl.BlockSpec(memory_space=pltpu.SMEM)
    sems = pltpu.SemaphoreType.DMA
    stat = pltpu.VMEM((8, 128), F32)
    stats = pltpu.VMEM((HEAD_PEERS, 8, 128), F32)
    gain = pltpu.VMEM((GAIN_ROWS, 128), F32)
    scratch = [
        pltpu.VMEM((TOKENS, QCOLS), BF16),
        pltpu.VMEM((TOKENS, QCOLS), BF16),
        pltpu.VMEM((TOKENS, QCOLS), BF16),
        pltpu.VMEM((TOKENS, QCOLS), BF16),
        pltpu.VMEM((TOKENS, QCOLS), F32),
        pltpu.VMEM((BLOCK, QCOLS), BF16),
        pltpu.VMEM((EXT, KCOLS), BF16),
        pltpu.VMEM((EXT, KCOLS), BF16),
        pltpu.VMEM((EXT, KCOLS), BF16),
        pltpu.VMEM((KCOLS, EXT), BF16),
        pltpu.VMEM((KCOLS, EXT), BF16),
        pltpu.VMEM((EXT, KCOLS), F32),
        pltpu.VMEM((EXT, KCOLS), F32),
        pltpu.VMEM((HALO, KCOLS), BF16),
        pltpu.VMEM((HALO, KCOLS), BF16),
        pltpu.VMEM((HALO, KCOLS), BF16),
        pltpu.VMEM((HALO, KCOLS), BF16),
        pltpu.VMEM((TOKENS, KCOLS), BF16),
        pltpu.VMEM((TOKENS, KCOLS), BF16),
        pltpu.VMEM((TOKENS, 128), F32),
        pltpu.VMEM((EXT, 128), F32),
        pltpu.VMEM((2, BLOCK, BLOCK), F32),
        pltpu.VMEM((16, 128), F32),
        pltpu.VMEM((HEAD_PEERS, 16, 128), F32),
        stat,
        stat,
        pltpu.VMEM((BLOCKS_HERE, 8, 128), F32),
        pltpu.VMEM((HEAD_PEERS, BLOCKS_HERE, 8, 128), F32),
        stat,
        stats,
        stat,
        stats,
        stat,
        stat,
        pltpu.VMEM((8, QCOLS), F32),
        pltpu.VMEM((8, KCOLS), F32),
        gain,
        pltpu.VMEM((4, GAIN_ROWS, 128), F32),
        pltpu.VMEM((4, GAIN_ROWS, 128), F32),
        pltpu.VMEM((2, GAIN_ROWS, 128), F32),
        sems((6,)),
        sems((2, BLOCKS_HERE)),
        sems((3,)),
        sems((3,)),
        sems((3,)),
        sems((3,)),
        sems((3, BLOCKS_HERE)),
        sems((3, BLOCKS_HERE)),
        sems((2, HALO_BLOCKS)),
        sems((2, HALO_BLOCKS)),
        sems((3,)),
        sems((3,)),
        sems((4,)),
        sems((4,)),
        sems((7,)),
        sems((7,)),
    ]
    shape = jax.ShapeDtypeStruct
    outs = pl.pallas_call(
        kernel,
        out_shape=[
            shape((TOKENS, QCOLS), BF16),
            shape((TOKENS, QCOLS), BF16),
            shape((TOKENS, KCOLS), BF16),
            shape((TOKENS, KCOLS), BF16),
            shape((1, QCOLS), F32),
            shape((1, KCOLS), F32),
        ],
        in_specs=[hbm] * 4 + [vmem] * 2 + [smem],
        out_specs=[hbm] * 4 + [vmem] * 2,
        scratch_shapes=scratch,
        compiler_params=pltpu.CompilerParams(
            collective_id=0, has_side_effects=True, vmem_limit_bytes=58 * 2**20
        ),
        cost_estimate=pl.CostEstimate(
            flops=8_000_000_000, bytes_accessed=10_000_000, transcendentals=5_000_000
        ),
    )(
        query_raw, key_raw, values, output_gradient,
        query_gain.reshape(1, QCOLS), key_norm_gain.reshape(1, KCOLS), block_docs,
    )
    return (*outs[:4], outs[4].reshape(QCOLS), outs[5].reshape(KCOLS))


def solution(mesh):
    placed = (
        P("ctx", "head"),
        P("ctx", "head"),
        P("ctx", "head"),
        P("ctx", "head"),
        P("head"),
        P("head"),
        P(),
    )
    return jax.shard_map(
        local,
        mesh=mesh,
        in_specs=placed,
        out_specs=(
            P("ctx", "head"),
            P("ctx", "head"),
            P("ctx", "head"),
            P("ctx", "head"),
            P("head"),
            P("head"),
        ),
        check_vma=False,
    )
```

time: 325 us -> 69.2 us (0.21)
  the two profiles are of different devices: /device:TPU:24 before, /device:TPU:4 now
where the time goes in v1:
time: 69.2 us; the launch traced here: 69.1 us
  Pallas kernels  61.1 us (88%)
  local copies, waits for them, and re-layouts  7.36 us (11%)
    pallas_call x1, Pallas kernels, local(): pl.pallas_call(kernel, out_shape=[shape((TOKENS, QCOLS), BF16), shape((TO...  61.1 us
    unnamed x16, local copies, waits for them, and re-layouts  7.36 us

profile of v1, /device:TPU:4, one launch (start us, length us, event | category | flops | bytes accessed | tf_op | source)
XLA Modules:
  0.0 69.1 jit_solution(10387447398094824369)
XLA Ops:
  0.6 61.1 %shard_map.118 = (bf16[1024,1024]{1,0:T(8,128)(2,1)}, bf16[1024,1024]{1,0:T(8,128)(2,1)}, bf16[1024,256]{1,0:T(8,128)(2,1)}, bf16[1024,256]{1,0:T(8,128)(2,1)}, f32[1,1024]{1,0:T(1,128)}, /*index=5*/f32[1,256]{1,0:T(1,128)}) custom-call(bf16[1024,1024]{1,0:T(8,128)(2,1)} %q_in.1, bf16[1024,256]{1,0:T(8,128)(2,1)} %k_in.1, bf16[1024,256]{1,0:T(8,128)(2,1)} %v_in.1, ...), custom_call_target="tpu_custom_call" | custom-call | flops 8000000000 | bytes 10000000 | tf_op jit(solution)/shard_map/pallas_call | solution.py:546
  61.7 0.0 copy-start
  61.7 3.2 %copy.19 = bf16[1024,1024]{1,0:T(8,128)(2,1)} copy(bf16[1024,1024]{1,0:T(8,128)(2,1)} %get-tuple-element.24) | data formatting | bytes 4194304
  64.9 0.0 copy-done
  64.9 0.0 copy-start.2
  64.9 0.0 copy-start.1
  64.9 1.3 %copy.20 = bf16[1024,1024]{1,0:T(8,128)(2,1)} copy(bf16[1024,1024]{1,0:T(8,128)(2,1)S(1)} %copy-done) | data formatting | bytes 4194304
  66.3 0.1 copy-done.2
  66.3 0.0 copy-start.3
  66.3 0.0 copy-start.4
  66.3 0.8 %copy.21 = bf16[1024,256]{1,0:T(8,128)(2,1)} copy(bf16[1024,256]{1,0:T(8,128)(2,1)S(1)} %copy-done.2) | data formatting | bytes 1048576
  67.1 0.0 copy-done.1
  67.1 0.8 %copy.22 = bf16[1024,256]{1,0:T(8,128)(2,1)} copy(bf16[1024,256]{1,0:T(8,128)(2,1)S(1)} %copy-done.1) | data formatting | bytes 1048576
  67.9 0.0 copy-done.3
  67.9 0.6 copy.23
  68.5 0.0 copy-done.4
  68.5 0.6 copy.24
Async XLA Ops:
  61.7 3.2 %copy-start = (bf16[1024,1024]{1,0:T(8,128)(2,1)S(1)}, bf16[1024,1024]{1,0:T(8,128)(2,1)}, u32[]{:S(2)}) copy-start(bf16[1024,1024]{1,0:T(8,128)(2,1)} %get-tuple-element.25) | copy-start | bytes 6291460
  64.9 1.4 %copy-start.2 = (bf16[1024,256]{1,0:T(8,128)(2,1)S(1)}, bf16[1024,256]{1,0:T(8,128)(2,1)}, u32[]{:S(2)}) copy-start(bf16[1024,256]{1,0:T(8,128)(2,1)} %get-tuple-element.26) | copy-start | bytes 1572868
  64.9 2.2 %copy-start.1 = (bf16[1024,256]{1,0:T(8,128)(2,1)S(1)}, bf16[1024,256]{1,0:T(8,128)(2,1)}, u32[]{:S(2)}) copy-start(bf16[1024,256]{1,0:T(8,128)(2,1)} %get-tuple-element.27) | copy-start | bytes 1572868
  66.3 1.6 %copy-start.3 = (f32[1,1024]{1,0:T(1,128)S(1)}, f32[1,1024]{1,0:T(1,128)}, u32[]{:S(2)}) copy-start(f32[1,1024]{1,0:T(1,128)} %get-tuple-element.16) | copy-start | bytes 12292
  66.3 2.2 %copy-start.4 = (f32[1,256]{1,0:T(1,128)S(1)}, f32[1,256]{1,0:T(1,128)}, u32[]{:S(2)}) copy-start(f32[1,256]{1,0:T(1,128)} %get-tuple-element.17) | copy-start | bytes 3076

commit v2 on v1

--- a/solution.py
+++ b/solution.py
@@ -28,6 +28,7 @@
 EXT = HALO + TOKENS
 GROUPS = 2
 GROUP = 4
+PAIR = 2
 HEADS = GROUPS * GROUP
 QCOLS = HEADS * HEAD_SIZE
 KCOLS = GROUPS * HEAD_SIZE
@@ -61,15 +62,15 @@
 
 def kernel(
     q_in, k_in, v_in, g_in, q_gain, k_gain, docs,
-    att_out, qg_out, kg_out, vg_out, qgain_out, kgain_out,
-    q_raw, go, att, qgrad, u_all, qn,
+    att, qgrad, kgrad, vgrad, qgain_out, kgain_out,
+    q_raw, go, u_all, qn,
     k_raw, vals, kn, k_t, v_t, dk, dv,
-    back_k, back_v, got_k, got_v, kgrad, vgrad,
+    back_k, back_v, got_k, got_v,
     q_col, k_col, tri,
     stat, stat_all, k_stat, halo_stat,
     inner, inner_all, kin, kin_all, hin, hin_all, hin_sum, hin_got,
-    q_acc, k_acc, gains, gains_x, gains_z, gains_y,
-    load_sem, out_sem, halo_send, halo_recv, stat_send, stat_recv,
+    q_acc, k_acc, products, gains, gains_x, gains_zy,
+    load_sem, halo_send, halo_recv, stat_send, stat_recv,
     inner_send, inner_recv, back_send, back_recv, kin_send, kin_recv,
     hin_send, hin_recv, gain_send, gain_recv,
 ):
@@ -84,10 +85,10 @@
     def at_x(r):
         return (y * 4 + z) * 4 + (x + r) % 4
 
-    def at_z(r):
-        return (y * 4 + (z + r) % 4) * 4 + x
-
-    at_y = (((y + 1) % 2) * 4 + z) * 4 + x
+    zy = y * 4 + z
+
+    def at_zy(r):
+        return ((zy + r) % 8) * 4 + x
 
     def at_head(r):
         return (head + r) % HEAD_PEERS
@@ -102,8 +103,9 @@
     for r in range(1, 4):
         pl.semaphore_signal(barrier, inc=1, device_id={"head": at_head(r)}, device_id_type=MESH)
         pl.semaphore_signal(barrier, inc=1, device_id={"ctx": at_x(r)}, device_id_type=MESH)
-        pl.semaphore_signal(barrier, inc=1, device_id={"ctx": at_z(r)}, device_id_type=MESH)
-    for other in (nxt, prv, at_y):
+    for r in range(1, 8):
+        pl.semaphore_signal(barrier, inc=1, device_id={"ctx": at_zy(r)}, device_id_type=MESH)
+    for other in (nxt, prv):
         pl.semaphore_signal(barrier, inc=1, device_id={"ctx": other}, device_id_type=MESH)
 
     own = pl.ds(HALO, TOKENS)
@@ -116,34 +118,24 @@
     load_v.start()
     load_g.start()
 
-    pl.semaphore_wait(barrier, 12)
-    tail = pl.ds(TOKENS - HALO, HALO)
-    front = pl.ds(0, HALO)
-    halo_copies = [
-        remote(k_in.at[tail], k_raw.at[front], halo_send.at[0], halo_recv.at[0], ctx=nxt),
-        remote(v_in.at[tail], vals.at[front], halo_send.at[1], halo_recv.at[1], ctx=nxt),
-    ]
-    for copy in halo_copies:
-        copy.start()
-
     load_k.wait()
     load_q.wait()
 
-    def squares(b, _):
-        rows = block_rows(b)
+    for b in range(BLOCKS_HERE):
+        rows = slice(b * BLOCK, (b + 1) * BLOCK)
         total = None
         for t in range(HEADS):
             part = q_raw[rows, cols(t)].astype(F32)
             total = part * part if total is None else total + part * part
-        stat[pl.ds(b, 1), :] = row_sums(total)
+        stat[b : b + 1] = row_sums(total)
+        rows = slice(HALO + b * BLOCK, HALO + (b + 1) * BLOCK)
         total = None
         for t in range(GROUPS):
-            part = k_raw[block_rows(b + HALO_BLOCKS), cols(t)].astype(F32)
+            part = k_raw[rows, cols(t)].astype(F32)
             total = part * part if total is None else total + part * part
-        stat[pl.ds(b + 8, 1), :] = row_sums(total)
-        return 0
-
-    lax.fori_loop(0, BLOCKS_HERE, squares, 0)
+        stat[b + 8 : b + 9] = row_sums(total)
+
+    pl.semaphore_wait(barrier, 15)
     stat_copies = [
         remote(stat, stat_all.at[head], stat_send.at[r - 1], stat_recv.at[r - 1], head=at_head(r))
         for r in range(1, 4)
@@ -151,6 +143,20 @@
     for copy in stat_copies:
         copy.start()
     stat_all[head] = stat[...]
+
+    def halo_copies(n):
+        there = pl.ds(TOKENS - HALO + n * BLOCK, BLOCK)
+        here = pl.ds(n * BLOCK, BLOCK)
+        return [
+            remote(k_in.at[there], k_raw.at[here], halo_send.at[n], halo_recv.at[n], ctx=nxt),
+            remote(
+                v_in.at[there], vals.at[here], halo_send.at[4 + n], halo_recv.at[4 + n], ctx=nxt
+            ),
+        ]
+
+    for n in reversed(range(HALO_BLOCKS)):
+        for copy in halo_copies(n):
+            copy.start()
 
     key_at = lax.broadcasted_iota(jnp.int32, (BLOCK, BLOCK), 0)
     query_at = lax.broadcasted_iota(jnp.int32, (BLOCK, BLOCK), 1)
@@ -174,7 +180,7 @@
         copy.wait_recv()
     total = stat_all[0] + stat_all[1] + stat_all[2] + stat_all[3]
     k_stat[...] = total[8:16]
-    relay = remote(k_stat, halo_stat, halo_send.at[2], halo_recv.at[2], ctx=nxt)
+    relay = remote(k_stat, halo_stat, halo_send.at[8], halo_recv.at[8], ctx=nxt)
     relay.start()
 
     q_scale = lax.rsqrt(total[0:8] / (QUERY_HEADS * HEAD_SIZE) + EPS)
@@ -197,15 +203,7 @@
     load_g.wait()
 
     def order(s):
-        return jnp.where(s < 3, s + 4, jnp.where(s < 7, s - 3, 7))
-
-    def att_copy(b):
-        rows = block_rows(b)
-        return pltpu.make_async_copy(att.at[rows], att_out.at[rows], out_sem.at[0, b])
-
-    def qgrad_copy(b):
-        rows = block_rows(b)
-        return pltpu.make_async_copy(qgrad.at[rows], qg_out.at[rows], out_sem.at[1, b])
+        return jnp.where(s < 3, s + 4, jnp.where(s == 3, 3, jnp.where(s < 7, s - 4, 7)))
 
     def inner_copies(b):
         return [
@@ -226,49 +224,66 @@
         for t in range(HEADS):
             unit = q_raw[rows, cols(t)].astype(F32) * scale
             qgrad[rows, cols(t)] = (scale * (u_all[rows, cols(t)] - unit * mean)).astype(BF16)
-        qgrad_copy(b).start()
-
-    def attend(b, biases, g):
+
+    def attend(b, biases):
         rows = block_rows(b)
         window = pl.ds(pl.multiple_of(b * BLOCK, BLOCK), WINDOW)
-        gc = cols(g)
-        queries = jnp.concatenate([qn[:, cols(g * GROUP + h)] for h in range(GROUP)], axis=0)
-        grads = jnp.concatenate([go[rows, cols(g * GROUP + h)] for h in range(GROUP)], axis=0)
-        scores = dot(kn[window, gc], queries, 1, 1)
-        first = jnp.concatenate([tri[0]] * GROUP, axis=1)
-        last = jnp.concatenate([tri[1]] * GROUP, axis=1)
-        parts = [scores[c * BLOCK : (c + 1) * BLOCK] for c in range(WINDOW_BLOCKS)]
-        parts[0] = parts[0] + first
-        parts[-1] = parts[-1] + last
-        top = None
-        for part, bias in zip(parts, biases):
-            here = jnp.max(part, axis=0, keepdims=True) + bias
-            top = here if top is None else jnp.maximum(top, here)
-        top = top * SCALE_LOG2
-        expo = [
-            jnp.exp2(part * SCALE_LOG2 - (top - bias)) for part, bias in zip(parts, biases)
-        ]
-        inverse = 1.0 / sum(jnp.sum(e, axis=0, keepdims=True) for e in expo)
-        weights = jnp.concatenate([e * inverse for e in expo], axis=0)
-        weights_low = weights.astype(BF16)
-        dweights = dot(vals[window, gc], grads, 1, 1)
-        delta = jnp.sum(weights * dweights, axis=0, keepdims=True)
-        dscores_low = (weights * (dweights - delta)).astype(BF16)
-        out_t = dot(v_t[gc, window], weights_low, 1, 0)
-        dquery_t = dot(k_t[gc, window], dscores_low, 1, 0)
-        dv[window, gc] += dot(weights_low, grads, 1, 0)
-        dk[window, gc] += dot(dscores_low, queries, 1, 0)
+        first = jnp.concatenate([tri[0]] * PAIR, axis=1)
+        last = jnp.concatenate([tri[1]] * PAIR, axis=1)
         scale = q_col[rows]
+
+        def products_in(g, h):
+            queries = jnp.concatenate([qn[:, cols(h + n)] for n in range(PAIR)], axis=0)
+            grads = jnp.concatenate([go[rows, cols(h + n)] for n in range(PAIR)], axis=0)
+            scores = dot(kn[window, cols(g)], queries, 1, 1)
+            dweights = dot(vals[window, cols(g)], grads, 1, 1)
+            return queries, grads, scores, dweights
+
+        def softmax(scores, dweights):
+            parts = [scores[c * BLOCK : (c + 1) * BLOCK] for c in range(WINDOW_BLOCKS)]
+            parts[0] = parts[0] + first
+            parts[-1] = parts[-1] + last
+            top = None
+            for part, bias in zip(parts, biases):
+                here = jnp.max(part, axis=0, keepdims=True) + bias
+                top = here if top is None else jnp.maximum(top, here)
+            top = top * SCALE_LOG2
+            expo = [
+                jnp.exp2(part * SCALE_LOG2 - (top - bias)) for part, bias in zip(parts, biases)
+            ]
+            inverse = 1.0 / sum(jnp.sum(e, axis=0, keepdims=True) for e in expo)
+            weights = jnp.concatenate([e * inverse for e in expo], axis=0)
+            delta = jnp.sum(weights * dweights, axis=0, keepdims=True)
+            return weights.astype(BF16), (weights * (dweights - delta)).astype(BF16)
+
+        def products_out(g, h, queries, grads, weights_low, dscores_low):
+            gc = cols(g)
+            out_t = dot(v_t[gc, window], weights_low, 1, 0)
+            dquery_t = dot(k_t[gc, window], dscores_low, 1, 0)
+            dv[window, gc] += dot(weights_low, grads, 1, 0)
+            dk[window, gc] += dot(dscores_low, queries, 1, 0)
+            product = None
+            for n in range(PAIR):
+                hc = cols(h + n)
+                att[rows, hc] = out_t[:, cols(n)].T.astype(BF16)
+                dquery = dquery_t[:, cols(n)].T * SCALE
+                onto = dquery * (q_raw[rows, hc].astype(F32) * scale)
+                q_acc[:, hc] += eight(onto)
+                gain = q_gain[:, hc]
+                u_all[rows, hc] = dquery * gain
+                product = onto * gain if product is None else product + onto * gain
+            return product
+
+        units = [(h // GROUP, h) for h in range(0, HEADS, PAIR)]
         product = None
-        for h in range(GROUP):
-            hc = cols(g * GROUP + h)
-            att[rows, hc] = out_t[:, cols(h)].T.astype(BF16)
-            dquery = dquery_t[:, cols(h)].T * SCALE
-            onto = dquery * (q_raw[rows, hc].astype(F32) * scale)
-            q_acc[:, hc] += eight(onto)
-            gain = q_gain[:, hc]
-            u_all[rows, hc] = dquery * gain
-            product = onto * gain if product is None else product + onto * gain
+        ahead = products_in(*units[0])
+        for n, unit in enumerate(units):
+            queries, grads, scores, dweights = ahead
+            if n + 1 < len(units):
+                ahead = products_in(*units[n + 1])
+            low = softmax(scores, dweights)
+            part = products_out(*unit, queries, grads, *low)
+            product = part if product is None else product + part
         return product
 
     def back_copies(b):
@@ -306,15 +321,22 @@
         b = order(s)
         rows = block_rows(b)
 
+        def take_halo(n):
+            for copy in halo_copies(n):
+                copy.wait_recv()
+            halo_scale = lax.rsqrt(halo_stat[...] / (KEY_VALUE_HEADS * HEAD_SIZE) + EPS)
+            norm_keys(n, halo_scale[n + HALO_BLOCKS : n + HALO_BLOCKS + 1])
+            turn_values(n, 0)
+
         @pl.when(s == 3)
         def _():
-            for copy in halo_copies:
-                copy.wait_recv()
             relay.wait_recv()
-            halo_scale = lax.rsqrt(halo_stat[...] / (KEY_VALUE_HEADS * HEAD_SIZE) + EPS)
-            for n in range(HALO_BLOCKS):
-                norm_keys(n, halo_scale[n + HALO_BLOCKS : n + HALO_BLOCKS + 1])
-            lax.fori_loop(0, HALO_BLOCKS, turn_values, 0)
+            take_halo(3)
+
+        @pl.when(s == 4)
+        def _():
+            for n in range(3):
+                take_halo(n)
 
         here = ctx * BLOCKS_HERE + b
         doc = docs[here]
@@ -329,35 +351,35 @@
             unit = q_raw[rows, cols(t)].astype(F32) * scale
             qn[:, cols(t)] = (unit * q_gain[:, cols(t)]).astype(BF16)
 
-        product = attend(b, biases, 0) + attend(b, biases, 1)
-        att_copy(b).start()
+        product = attend(b, biases)
         tile = jnp.broadcast_to(row_sums(product), (8, 128))
         inner[b] = tile
         inner_all[head, b] = tile
         for copy in inner_copies(b):
             copy.start()
 
-        @pl.when((s >= 3) & (s < 7))
+        @pl.when((s >= 4) & (s < 7))
         def _():
-            send_back(s - 3)
+            send_back(s - 4)
 
         @pl.when(s == 6)
         def _():
+            send_back(3)
             hin_all[head] = hin[...]
             for copy in hin_copies:
                 copy.start()
 
-        @pl.when((s >= 1) & (s < 7))
+        @pl.when(s >= 4)
         def _():
-            finish_queries(order(s - 1))
+            finish_queries(order(s - 4))
 
         return 0
 
     hin[...] = jnp.zeros_like(hin)
     lax.fori_loop(0, BLOCKS_HERE, step, 0)
 
-    def own_keys(b, _):
-        rows = block_rows(b + HALO_BLOCKS)
+    for b in range(BLOCKS_HERE):
+        rows = slice(HALO + b * BLOCK, HALO + (b + 1) * BLOCK)
         scale = k_col[rows]
         product = None
         for t in range(GROUPS):
@@ -365,10 +387,8 @@
             k_acc[:, cols(t)] += eight(onto)
             gain = k_gain[:, cols(t)]
             product = onto * gain if product is None else product + onto * gain
-        kin[pl.ds(b, 1), :] = row_sums(product)
-        return 0
-
-    lax.fori_loop(0, BLOCKS_HERE, own_keys, 0)
+        products[b] = product
+
     for t in range(HEADS):
         gains[t : t + 1] = jnp.sum(q_acc[:, cols(t)], axis=0, keepdims=True)
     for t in range(GROUPS):
@@ -381,6 +401,8 @@
     for copy in x_copies:
         copy.start()
     gains_x[x] = gains[...]
+    for b in range(BLOCKS_HERE):
+        kin[b : b + 1] = row_sums(products[b])
     kin_copies = exchange(kin, kin_all, kin_send, kin_recv)
     for copy in kin_copies:
         copy.start()
@@ -392,28 +414,23 @@
     hin_back = remote(hin_sum, hin_got, hin_send.at[3], hin_recv.at[3], ctx=prv)
     hin_back.start()
 
-    finish_queries(3)
-
     for copy in x_copies:
         copy.wait_recv()
-    mine = gains_x[0] + gains_x[1] + gains_x[2] + gains_x[3]
-    gains_z[z] = mine
-    z_copies = [
+    gains_zy[zy] = gains_x[0] + gains_x[1] + gains_x[2] + gains_x[3]
+    zy_copies = [
         remote(
-            gains_z.at[z], gains_z.at[z], gain_send.at[r + 2], gain_recv.at[r + 2], ctx=at_z(r)
+            gains_zy.at[zy], gains_zy.at[zy], gain_send.at[r + 2], gain_recv.at[r + 2], ctx=at_zy(r)
         )
-        for r in range(1, 4)
+        for r in range(1, 8)
     ]
-    for copy in z_copies:
+    for copy in zy_copies:
         copy.start()
 
-    finish_queries(7)
-
-    for copy in z_copies:
-        copy.wait_recv()
-    gains_y[y] = gains_z[0] + gains_z[1] + gains_z[2] + gains_z[3]
-    y_copy = remote(gains_y.at[y], gains_y.at[y], gain_send.at[6], gain_recv.at[6], ctx=at_y)
-    y_copy.start()
+    def finish_later(s, _):
+        finish_queries(order(s))
+        return 0
+
+    lax.fori_loop(4, BLOCKS_HERE, finish_later, 0)
 
     for n in range(HALO_BLOCKS):
         for copy in back_copies(n):
@@ -421,8 +438,6 @@
     split = TOKENS - HALO
     vgrad[0:split] = dv[HALO : HALO + split].astype(BF16)
     vgrad[split:] = (dv[HALO + split :] + got_v[...].astype(F32)).astype(BF16)
-    v_copy = pltpu.make_async_copy(vgrad, vg_out, load_sem.at[4])
-    v_copy.start()
 
     for copy in kin_copies:
         copy.wait_recv()
@@ -445,39 +460,48 @@
             unit = k_raw[rows, cols(t)].astype(F32) * scale
             grad = scale * (dkey * k_gain[:, cols(t)] - unit * mean)
             kgrad[there, cols(t)] = grad.astype(BF16)
-    k_copy = pltpu.make_async_copy(kgrad, kg_out, load_sem.at[5])
-    k_copy.start()
-
-    y_copy.wait_recv()
-    summed = gains_y[0] + gains_y[1]
+
+    for copy in zy_copies:
+        copy.wait_recv()
+    summed = gains_zy[0]
+    for n in range(1, 8):
+        summed = summed + gains_zy[n]
     for t in range(HEADS):
         qgain_out[:, cols(t)] = summed[t : t + 1]
     for t in range(GROUPS):
         kgain_out[:, cols(t)] = summed[HEADS + t : HEADS + t + 1]
 
     for copy in (
-        halo_copies + [relay] + stat_copies + hin_copies + [hin_back] + kin_copies
-        + x_copies + z_copies + [y_copy]
+        [relay] + stat_copies + hin_copies + [hin_back] + kin_copies + x_copies + zy_copies
     ):
         copy.wait_send()
     for n in range(HALO_BLOCKS):
-        for copy in back_copies(n):
+        for copy in halo_copies(n) + back_copies(n):
             copy.wait_send()
 
     def drain(b, _):
         for copy in inner_copies(b):
             copy.wait_send()
-        att_copy(b).wait()
-        qgrad_copy(b).wait()
         return 0
 
     lax.fori_loop(0, BLOCKS_HERE, drain, 0)
-    v_copy.wait()
-    k_copy.wait()
+
+
+def write(*refs):
+    *pairs, sem = refs
+    half = len(pairs) // 2
+    copies = [
+        pltpu.make_async_copy(src, dst, sem.at[n])
+        for n, (src, dst) in enumerate(zip(pairs[:half], pairs[half:]))
+    ]
+    for copy in copies:
+        copy.start()
+    for copy in copies:
+        copy.wait()
 
 
 def local(query_raw, key_raw, values, output_gradient, query_gain, key_norm_gain, block_docs):
-    hbm = pl.BlockSpec(memory_space=pl.ANY)
+    hbm = pl.BlockSpec(memory_space=pltpu.HBM)
     vmem = pl.BlockSpec(memory_space=pltpu.VMEM)
     smem = pl.BlockSpec(memory_space=pltpu.SMEM)
     sems = pltpu.SemaphoreType.DMA
@@ -485,8 +509,6 @@
     stats = pltpu.VMEM((HEAD_PEERS, 8, 128), F32)
     gain = pltpu.VMEM((GAIN_ROWS, 128), F32)
     scratch = [
-        pltpu.VMEM((TOKENS, QCOLS), BF16),
-        pltpu.VMEM((TOKENS, QCOLS), BF16),
         pltpu.VMEM((TOKENS, QCOLS), BF16),
         pltpu.VMEM((TOKENS, QCOLS), BF16),
         pltpu.VMEM((TOKENS, QCOLS), F32),
@@ -502,8 +524,6 @@
         pltpu.VMEM((HALO, KCOLS), BF16),
         pltpu.VMEM((HALO, KCOLS), BF16),
         pltpu.VMEM((HALO, KCOLS), BF16),
-        pltpu.VMEM((TOKENS, KCOLS), BF16),
-        pltpu.VMEM((TOKENS, KCOLS), BF16),
         pltpu.VMEM((TOKENS, 128), F32),
         pltpu.VMEM((EXT, 128), F32),
         pltpu.VMEM((2, BLOCK, BLOCK), F32),
@@ -521,14 +541,13 @@
         stat,
         pltpu.VMEM((8, QCOLS), F32),
         pltpu.VMEM((8, KCOLS), F32),
+        pltpu.VMEM((BLOCKS_HERE, 128, 128), F32),
         gain,
         pltpu.VMEM((4, GAIN_ROWS, 128), F32),
-        pltpu.VMEM((4, GAIN_ROWS, 128), F32),
-        pltpu.VMEM((2, GAIN_ROWS, 128), F32),
-        sems((6,)),
-        sems((2, BLOCKS_HERE)),
-        sems((3,)),
-        sems((3,)),
+        pltpu.VMEM((8, GAIN_ROWS, 128), F32),
+        sems((4,)),
+        sems((9,)),
+        sems((9,)),
         sems((3,)),
         sems((3,)),
         sems((3, BLOCKS_HERE)),
@@ -539,25 +558,25 @@
         sems((3,)),
         sems((4,)),
         sems((4,)),
-        sems((7,)),
-        sems((7,)),
+        sems((10,)),
+        sems((10,)),
     ]
-    shape = jax.ShapeDtypeStruct
-    outs = pl.pallas_call(
+    shapes = [
+        ((TOKENS, QCOLS), BF16),
+        ((TOKENS, QCOLS), BF16),
+        ((TOKENS, KCOLS), BF16),
+        ((TOKENS, KCOLS), BF16),
+        ((1, QCOLS), F32),
+        ((1, KCOLS), F32),
+    ]
+    held = pl.pallas_call(
         kernel,
-        out_shape=[
-            shape((TOKENS, QCOLS), BF16),
-            shape((TOKENS, QCOLS), BF16),
-            shape((TOKENS, KCOLS), BF16),
-            shape((TOKENS, KCOLS), BF16),
-            shape((1, QCOLS), F32),
-            shape((1, KCOLS), F32),
-        ],
+        out_shape=[pltpu.VMEM(*shape) for shape in shapes],
         in_specs=[hbm] * 4 + [vmem] * 2 + [smem],
-        out_specs=[hbm] * 4 + [vmem] * 2,
+        out_specs=[vmem] * 6,
         scratch_shapes=scratch,
         compiler_params=pltpu.CompilerParams(
-            collective_id=0, has_side_effects=True, vmem_limit_bytes=58 * 2**20
+            collective_id=0, has_side_effects=True, vmem_limit_bytes=56 * 2**20
         ),
         cost_estimate=pl.CostEstimate(
             flops=8_000_000_000, bytes_accessed=10_000_000, transcendentals=5_000_000
@@ -566,6 +585,14 @@
         query_raw, key_raw, values, output_gradient,
         query_gain.reshape(1, QCOLS), key_norm_gain.reshape(1, KCOLS), block_docs,
     )
+    outs = pl.pallas_call(
+        write,
+        out_shape=[jax.ShapeDtypeStruct(*shape) for shape in shapes],
+        in_specs=[vmem] * 6,
+        out_specs=[hbm] * 6,
+        scratch_shapes=[sems((6,))],
+        compiler_params=pltpu.CompilerParams(vmem_limit_bytes=16 * 2**20),
+    )(*[pltpu.with_memory_space_constraint(x, pltpu.VMEM) for x in held])
     return (*outs[:4], outs[4].reshape(QCOLS), outs[5].reshape(KCOLS))
 
 

time: 69.2 us -> 50.1 us (0.72)
  the two profiles are of different devices: /device:TPU:4 before, /device:TPU:6 now
where the time goes in v2:
time: 50.1 us; the launch traced here: 49.9 us
  Pallas kernels  49.3 us (98%)
  between operations  0.64 us (1%)
    pallas_call x1, Pallas kernels, local(): pl.pallas_call(kernel, out_shape=[pltpu.VMEM(*shape) for shape in shapes]...  46.9 us
    pallas_call x1, Pallas kernels, local(): pl.pallas_call(write, out_shape=[jax.ShapeDtypeStruct(*shape) for shape i...  2.39 us

profile of v2, /device:TPU:6, one launch (start us, length us, event | category | flops | bytes accessed | tf_op | source)
XLA Modules:
  0.0 49.9 jit_solution(4805922028346841358)
XLA Ops:
  0.6 46.9 %shard_map.118 = (bf16[1024,1024]{1,0:T(8,128)(2,1)S(1)}, bf16[1024,1024]{1,0:T(8,128)(2,1)S(1)}, bf16[1024,256]{1,0:T(8,128)(2,1)S(1)}, bf16[1024,256]{1,0:T(8,...) custom-call(bf16[1024,1024]{1,0:T(8,128)(2,1)} %q_in.1, bf16[1024,256]{1,0:T(8,128)(2,1)} %k_in.1, ...), custom_call_target="tpu_custom_call" | custom-call | flops 8000000000 | bytes 10000000 | tf_op jit(solution)/shard_map/pallas_call | solution.py:572
  47.6 2.4 %shard_map.119 = (bf16[1024,1024]{1,0:T(8,128)(2,1)}, bf16[1024,1024]{1,0:T(8,128)(2,1)}, bf16[1024,256]{1,0:T(8,128)(2,1)}, bf16[1024,256]{1,0:T(8,128)(2,1)}, f32[1,1024]{1,0:T(1,128)}, /*index=5*/f32[1,256]{1,0:T(1,128)}) custom-call(bf16[1024,1024]{1,0:T(8,128)(2,1)S(1)} %get-tuple-element.18.refs_0_, bf16[1024,1024]{1,0:T(8,128)(2,1)S(1)} %get-tuple-element.19.refs_1_, ...), custom_call_target="tpu_custom_call" | custom-call | tf_op jit(solution)/shard_map/pallas_call | solution.py:588

commit v3 on v2

--- a/solution.py
+++ b/solution.py
@@ -29,6 +29,7 @@
 GROUPS = 2
 GROUP = 4
 PAIR = 2
+QUERY_PIECES = 4
 HEADS = GROUPS * GROUP
 QCOLS = HEADS * HEAD_SIZE
 KCOLS = GROUPS * HEAD_SIZE
@@ -66,7 +67,7 @@
     q_raw, go, u_all, qn,
     k_raw, vals, kn, k_t, v_t, dk, dv,
     back_k, back_v, got_k, got_v,
-    q_col, k_col, tri,
+    q_col, k_col, tri, near, far,
     stat, stat_all, k_stat, halo_stat,
     inner, inner_all, kin, kin_all, hin, hin_all, hin_sum, hin_got,
     q_acc, k_acc, products, gains, gains_x, gains_zy,
@@ -99,6 +100,18 @@
             device_id=where, device_id_type=MESH,
         )
 
+    own = pl.ds(HALO, TOKENS)
+    load_k = pltpu.make_async_copy(k_in, k_raw.at[own], load_sem.at[0])
+    load_v = pltpu.make_async_copy(v_in, vals.at[own], load_sem.at[1])
+    load_g = pltpu.make_async_copy(g_in, go, load_sem.at[2])
+    load_q = []
+    for n in range(QUERY_PIECES):
+        rows = pl.ds(n * (TOKENS // QUERY_PIECES), TOKENS // QUERY_PIECES)
+        load_q.append(pltpu.make_async_copy(q_in.at[rows], q_raw.at[rows], load_sem.at[3 + n]))
+    for copy in load_q:
+        copy.start()
+    load_k.start()
+
     barrier = pltpu.get_barrier_semaphore()
     for r in range(1, 4):
         pl.semaphore_signal(barrier, inc=1, device_id={"head": at_head(r)}, device_id_type=MESH)
@@ -107,42 +120,6 @@
         pl.semaphore_signal(barrier, inc=1, device_id={"ctx": at_zy(r)}, device_id_type=MESH)
     for other in (nxt, prv):
         pl.semaphore_signal(barrier, inc=1, device_id={"ctx": other}, device_id_type=MESH)
-
-    own = pl.ds(HALO, TOKENS)
-    load_k = pltpu.make_async_copy(k_in, k_raw.at[own], load_sem.at[0])
-    load_q = pltpu.make_async_copy(q_in, q_raw, load_sem.at[1])
-    load_v = pltpu.make_async_copy(v_in, vals.at[own], load_sem.at[2])
-    load_g = pltpu.make_async_copy(g_in, go, load_sem.at[3])
-    load_k.start()
-    load_q.start()
-    load_v.start()
-    load_g.start()
-
-    load_k.wait()
-    load_q.wait()
-
-    for b in range(BLOCKS_HERE):
-        rows = slice(b * BLOCK, (b + 1) * BLOCK)
-        total = None
-        for t in range(HEADS):
-            part = q_raw[rows, cols(t)].astype(F32)
-            total = part * part if total is None else total + part * part
-        stat[b : b + 1] = row_sums(total)
-        rows = slice(HALO + b * BLOCK, HALO + (b + 1) * BLOCK)
-        total = None
-        for t in range(GROUPS):
-            part = k_raw[rows, cols(t)].astype(F32)
-            total = part * part if total is None else total + part * part
-        stat[b + 8 : b + 9] = row_sums(total)
-
-    pl.semaphore_wait(barrier, 15)
-    stat_copies = [
-        remote(stat, stat_all.at[head], stat_send.at[r - 1], stat_recv.at[r - 1], head=at_head(r))
-        for r in range(1, 4)
-    ]
-    for copy in stat_copies:
-        copy.start()
-    stat_all[head] = stat[...]
 
     def halo_copies(n):
         there = pl.ds(TOKENS - HALO + n * BLOCK, BLOCK)
@@ -154,14 +131,48 @@
             ),
         ]
 
-    for n in reversed(range(HALO_BLOCKS)):
-        for copy in halo_copies(n):
-            copy.start()
+    def send_halo(*chunks):
+        for n in chunks:
+            for copy in halo_copies(n):
+                copy.start()
+
+    for b in range(BLOCKS_HERE):
+        if b % (BLOCKS_HERE // QUERY_PIECES) == 0:
+            load_q[b * QUERY_PIECES // BLOCKS_HERE].wait()
+        rows = slice(b * BLOCK, (b + 1) * BLOCK)
+        total = None
+        for t in range(HEADS):
+            part = q_raw[rows, cols(t)].astype(F32)
+            total = part * part if total is None else total + part * part
+        stat[b : b + 1] = row_sums(total)
+    load_k.wait()
+    load_v.start()
+    load_g.start()
+    for b in range(BLOCKS_HERE):
+        rows = slice(HALO + b * BLOCK, HALO + (b + 1) * BLOCK)
+        total = None
+        for t in range(GROUPS):
+            part = k_raw[rows, cols(t)].astype(F32)
+            total = part * part if total is None else total + part * part
+        stat[b + 8 : b + 9] = row_sums(total)
+
+    pl.semaphore_wait(barrier, 15)
+    stat_copies = [
+        remote(stat, stat_all.at[head], stat_send.at[r - 1], stat_recv.at[r - 1], head=at_head(r))
+        for r in range(1, 4)
+    ]
+    for copy in stat_copies:
+        copy.start()
+    stat_all[head] = stat[...]
+
+    send_halo(3)
 
     key_at = lax.broadcasted_iota(jnp.int32, (BLOCK, BLOCK), 0)
     query_at = lax.broadcasted_iota(jnp.int32, (BLOCK, BLOCK), 1)
-    tri[0] = jnp.where(key_at > query_at, 0.0, NEGATIVE)
-    tri[1] = jnp.where(key_at <= query_at, 0.0, NEGATIVE)
+    lower = jnp.where(key_at <= query_at, 1.0, 0.0)
+    tri[...] = jnp.concatenate([lower] * PAIR, axis=1)
+    near[...] = jnp.concatenate([lower] * PAIR, axis=1).astype(BF16)
+    far[...] = (1.0 - jnp.concatenate([lower] * PAIR, axis=1)).astype(BF16)
     dk[...] = jnp.zeros_like(dk)
     dv[...] = jnp.zeros_like(dv)
     q_acc[...] = jnp.zeros_like(q_acc)
@@ -182,6 +193,7 @@
     k_stat[...] = total[8:16]
     relay = remote(k_stat, halo_stat, halo_send.at[8], halo_recv.at[8], ctx=nxt)
     relay.start()
+    send_halo(2, 1, 0)
 
     q_scale = lax.rsqrt(total[0:8] / (QUERY_HEADS * HEAD_SIZE) + EPS)
     for b in range(BLOCKS_HERE):
@@ -225,11 +237,10 @@
             unit = q_raw[rows, cols(t)].astype(F32) * scale
             qgrad[rows, cols(t)] = (scale * (u_all[rows, cols(t)] - unit * mean)).astype(BF16)
 
-    def attend(b, biases):
+    def attend(b, biases, qn):
         rows = block_rows(b)
         window = pl.ds(pl.multiple_of(b * BLOCK, BLOCK), WINDOW)
-        first = jnp.concatenate([tri[0]] * PAIR, axis=1)
-        last = jnp.concatenate([tri[1]] * PAIR, axis=1)
+        lower = tri[...] > 0.5
         scale = q_col[rows]
 
         def products_in(g, h):
@@ -239,22 +250,33 @@
             dweights = dot(vals[window, cols(g)], grads, 1, 1)
             return queries, grads, scores, dweights
 
+        def fold(tiles, bias):
+            tiles = [tiles[c * BLOCK : (c + 1) * BLOCK] for c in range(WINDOW_BLOCKS)]
+            return [jnp.where(lower, tiles[-1], tiles[0] + bias)] + tiles[1:-1]
+
+        def unfold(tiles):
+            low = [tile.astype(BF16) for tile in tiles]
+            return jnp.concatenate([low[0] * far[...]] + low[1:] + [low[0] * near[...]], axis=0)
+
         def softmax(scores, dweights):
-            parts = [scores[c * BLOCK : (c + 1) * BLOCK] for c in range(WINDOW_BLOCKS)]
-            parts[0] = parts[0] + first
-            parts[-1] = parts[-1] + last
+            parts = fold(scores, biases[0])
+            dparts = fold(dweights, 0.0)
+            shifts = [0.0] + biases[1:-1]
             top = None
-            for part, bias in zip(parts, biases):
-                here = jnp.max(part, axis=0, keepdims=True) + bias
+            for part, shift in zip(parts, shifts):
+                here = jnp.max(part, axis=0, keepdims=True) + shift
                 top = here if top is None else jnp.maximum(top, here)
             top = top * SCALE_LOG2
             expo = [
-                jnp.exp2(part * SCALE_LOG2 - (top - bias)) for part, bias in zip(parts, biases)
+                jnp.exp2(part * SCALE_LOG2 - (top - shift)) for part, shift in zip(parts, shifts)
             ]
             inverse = 1.0 / sum(jnp.sum(e, axis=0, keepdims=True) for e in expo)
-            weights = jnp.concatenate([e * inverse for e in expo], axis=0)
-            delta = jnp.sum(weights * dweights, axis=0, keepdims=True)
-            return weights.astype(BF16), (weights * (dweights - delta)).astype(BF16)
+            weights = [e * inverse for e in expo]
+            delta = sum(
+                jnp.sum(w * d, axis=0, keepdims=True) for w, d in zip(weights, dparts)
+            )
+            dscores = [w * (d - delta) for w, d in zip(weights, dparts)]
+            return unfold(weights), unfold(dscores)
 
         def products_out(g, h, queries, grads, weights_low, dscores_low):
             gc = cols(g)
@@ -293,7 +315,7 @@
             remote(back_v.at[rows], got_v.at[rows], back_send.at[1, b], back_recv.at[1, b], ctx=prv),
         ]
 
-    def send_back(b):
+    def send_back(b, start=True):
         rows = block_rows(b)
         scale = k_col[rows]
         product = None
@@ -305,8 +327,9 @@
             back_v[rows, cols(t)] = dv[rows, cols(t)].astype(BF16)
             gain = k_gain[:, cols(t)]
             product = onto * gain if product is None else product + onto * gain
-        for copy in back_copies(b):
-            copy.start()
+        if start:
+            for copy in back_copies(b):
+                copy.start()
         hin[pl.ds(b, 1), :] = row_sums(product)
 
     def exchange(src, dst, send, recv):
@@ -317,27 +340,22 @@
 
     hin_copies = exchange(hin, hin_all, hin_send, hin_recv)
 
-    def step(s, _):
+    def norm_queries(b, slot):
+        rows = block_rows(b)
+        scale = q_col[rows]
+        for t in range(HEADS):
+            unit = q_raw[rows, cols(t)].astype(F32) * scale
+            qn[slot, :, cols(t)] = (unit * q_gain[:, cols(t)]).astype(BF16)
+
+    def take_halo(n):
+        for copy in halo_copies(n):
+            copy.wait_recv()
+        halo_scale = lax.rsqrt(halo_stat[...] / (KEY_VALUE_HEADS * HEAD_SIZE) + EPS)
+        norm_keys(n, halo_scale[n + HALO_BLOCKS : n + HALO_BLOCKS + 1])
+        turn_values(n, 0)
+
+    def work(s):
         b = order(s)
-        rows = block_rows(b)
-
-        def take_halo(n):
-            for copy in halo_copies(n):
-                copy.wait_recv()
-            halo_scale = lax.rsqrt(halo_stat[...] / (KEY_VALUE_HEADS * HEAD_SIZE) + EPS)
-            norm_keys(n, halo_scale[n + HALO_BLOCKS : n + HALO_BLOCKS + 1])
-            turn_values(n, 0)
-
-        @pl.when(s == 3)
-        def _():
-            relay.wait_recv()
-            take_halo(3)
-
-        @pl.when(s == 4)
-        def _():
-            for n in range(3):
-                take_halo(n)
-
         here = ctx * BLOCKS_HERE + b
         doc = docs[here]
         biases = []
@@ -345,38 +363,46 @@
             there = here - HALO_BLOCKS + c
             same = (docs[jnp.maximum(there, 0)] == doc) & (there >= 0)
             biases.append(jnp.where(same, 0.0, NEGATIVE))
-
-        scale = q_col[rows]
-        for t in range(HEADS):
-            unit = q_raw[rows, cols(t)].astype(F32) * scale
-            qn[:, cols(t)] = (unit * q_gain[:, cols(t)]).astype(BF16)
-
-        product = attend(b, biases)
+        product = attend(b, biases, qn.at[s % 2])
+        norm_queries(order(s + 1), (s + 1) % 2)
         tile = jnp.broadcast_to(row_sums(product), (8, 128))
         inner[b] = tile
         inner_all[head, b] = tile
         for copy in inner_copies(b):
             copy.start()
 
-        @pl.when((s >= 4) & (s < 7))
+    def early(s, _):
+        @pl.when(s == 3)
+        def _():
+            relay.wait_recv()
+            take_halo(3)
+
+        work(s)
+        return 0
+
+    def late(s, _):
+        finish_queries(order(s - 4))
+        work(s)
+
+        @pl.when(s < 7)
         def _():
             send_back(s - 4)
 
         @pl.when(s == 6)
         def _():
-            send_back(3)
+            send_back(3, start=False)
             hin_all[head] = hin[...]
             for copy in hin_copies:
                 copy.start()
 
-        @pl.when(s >= 4)
-        def _():
-            finish_queries(order(s - 4))
-
         return 0
 
     hin[...] = jnp.zeros_like(hin)
-    lax.fori_loop(0, BLOCKS_HERE, step, 0)
+    norm_queries(order(0), 0)
+    lax.fori_loop(0, 4, early, 0)
+    for n in range(3):
+        take_halo(n)
+    lax.fori_loop(4, BLOCKS_HERE, late, 0)
 
     for b in range(BLOCKS_HERE):
         rows = slice(HALO + b * BLOCK, HALO + (b + 1) * BLOCK)
@@ -414,6 +440,8 @@
     hin_back = remote(hin_sum, hin_got, hin_send.at[3], hin_recv.at[3], ctx=prv)
     hin_back.start()
 
+    last_k, last_v = back_copies(HALO_BLOCKS - 1)
+    last_k.start()
     for copy in x_copies:
         copy.wait_recv()
     gains_zy[zy] = gains_x[0] + gains_x[1] + gains_x[2] + gains_x[3]
@@ -425,6 +453,7 @@
     ]
     for copy in zy_copies:
         copy.start()
+    last_v.start()
 
     def finish_later(s, _):
         finish_queries(order(s))
@@ -512,7 +541,7 @@
         pltpu.VMEM((TOKENS, QCOLS), BF16),
         pltpu.VMEM((TOKENS, QCOLS), BF16),
         pltpu.VMEM((TOKENS, QCOLS), F32),
-        pltpu.VMEM((BLOCK, QCOLS), BF16),
+        pltpu.VMEM((2, BLOCK, QCOLS), BF16),
         pltpu.VMEM((EXT, KCOLS), BF16),
         pltpu.VMEM((EXT, KCOLS), BF16),
         pltpu.VMEM((EXT, KCOLS), BF16),
@@ -526,7 +555,9 @@
         pltpu.VMEM((HALO, KCOLS), BF16),
         pltpu.VMEM((TOKENS, 128), F32),
         pltpu.VMEM((EXT, 128), F32),
-        pltpu.VMEM((2, BLOCK, BLOCK), F32),
+        pltpu.VMEM((BLOCK, PAIR * BLOCK), F32),
+        pltpu.VMEM((BLOCK, PAIR * BLOCK), BF16),
+        pltpu.VMEM((BLOCK, PAIR * BLOCK), BF16),
         pltpu.VMEM((16, 128), F32),
         pltpu.VMEM((HEAD_PEERS, 16, 128), F32),
         stat,
@@ -545,7 +576,7 @@
         gain,
         pltpu.VMEM((4, GAIN_ROWS, 128), F32),
         pltpu.VMEM((8, GAIN_ROWS, 128), F32),
-        sems((4,)),
+        sems((3 + QUERY_PIECES,)),
         sems((9,)),
         sems((9,)),
         sems((3,)),

time: 50.1 us -> 48.5 us (0.968)
  the two profiles are of different devices: /device:TPU:6 before, /device:TPU:4 now
where the time goes in v3:
time: 48.5 us; the launch traced here: 48.3 us
  Pallas kernels  47.7 us (98%)
  between operations  0.64 us (1%)
    pallas_call x1, Pallas kernels, local(): pl.pallas_call(kernel, out_shape=[pltpu.VMEM(*shape) for shape in shapes]...  45.3 us
    pallas_call x1, Pallas kernels, local(): pl.pallas_call(write, out_shape=[jax.ShapeDtypeStruct(*shape) for shape i...  2.39 us

profile of v3, /device:TPU:4, one launch (start us, length us, event | category | flops | bytes accessed | tf_op | source)
XLA Modules:
  0.0 48.3 jit_solution(10465040323922303985)
XLA Ops:
  0.6 45.3 %shard_map.118 = (bf16[1024,1024]{1,0:T(8,128)(2,1)S(1)}, bf16[1024,1024]{1,0:T(8,128)(2,1)S(1)}, bf16[1024,256]{1,0:T(8,128)(2,1)S(1)}, bf16[1024,256]{1,0:T(8,...) custom-call(bf16[1024,1024]{1,0:T(8,128)(2,1)} %q_in.1, bf16[1024,256]{1,0:T(8,128)(2,1)} %k_in.1, ...), custom_call_target="tpu_custom_call" | custom-call | flops 8000000000 | bytes 10000000 | tf_op jit(solution)/shard_map/pallas_call | solution.py:603
  45.9 2.4 %shard_map.119 = (bf16[1024,1024]{1,0:T(8,128)(2,1)}, bf16[1024,1024]{1,0:T(8,128)(2,1)}, bf16[1024,256]{1,0:T(8,128)(2,1)}, bf16[1024,256]{1,0:T(8,128)(2,1)}, f32[1,1024]{1,0:T(1,128)}, /*index=5*/f32[1,256]{1,0:T(1,128)}) custom-call(bf16[1024,1024]{1,0:T(8,128)(2,1)S(1)} %get-tuple-element.18.refs_0_, bf16[1024,1024]{1,0:T(8,128)(2,1)S(1)} %get-tuple-element.19.refs_1_, ...), custom_call_target="tpu_custom_call" | custom-call | tf_op jit(solution)/shard_map/pallas_call | solution.py:619

commit v4 on v3

--- a/solution.py
+++ b/solution.py
@@ -62,8 +62,9 @@
 
 
 def kernel(
-    q_in, k_in, v_in, g_in, q_gain, k_gain, docs,
+    q_in, k_in, v_in, g_in, q_gain_in, k_gain_in, docs_in,
     att, qgrad, kgrad, vgrad, qgain_out, kgain_out,
+    q_gain, k_gain, docs,
     q_raw, go, u_all, qn,
     k_raw, vals, kn, k_t, v_t, dk, dv,
     back_k, back_v, got_k, got_v,
@@ -111,6 +112,13 @@
     for copy in load_q:
         copy.start()
     load_k.start()
+    load_small = [
+        pltpu.make_async_copy(q_gain_in, q_gain, load_sem.at[3 + QUERY_PIECES]),
+        pltpu.make_async_copy(k_gain_in, k_gain, load_sem.at[4 + QUERY_PIECES]),
+        pltpu.make_async_copy(docs_in, docs, load_sem.at[5 + QUERY_PIECES]),
+    ]
+    for copy in load_small:
+        copy.start()
 
     barrier = pltpu.get_barrier_semaphore()
     for r in range(1, 4):
@@ -209,6 +217,8 @@
             kn[rows, cols(t)] = normed
             k_t[cols(t), rows] = normed.T
 
+    for copy in load_small:
+        copy.wait()
     k_scale = lax.rsqrt(total[8:16] / (KEY_VALUE_HEADS * HEAD_SIZE) + EPS)
     for b in range(BLOCKS_HERE):
         norm_keys(b + HALO_BLOCKS, k_scale[b : b + 1])
@@ -532,12 +542,14 @@
 def local(query_raw, key_raw, values, output_gradient, query_gain, key_norm_gain, block_docs):
     hbm = pl.BlockSpec(memory_space=pltpu.HBM)
     vmem = pl.BlockSpec(memory_space=pltpu.VMEM)
-    smem = pl.BlockSpec(memory_space=pltpu.SMEM)
     sems = pltpu.SemaphoreType.DMA
     stat = pltpu.VMEM((8, 128), F32)
     stats = pltpu.VMEM((HEAD_PEERS, 8, 128), F32)
     gain = pltpu.VMEM((GAIN_ROWS, 128), F32)
     scratch = [
+        pltpu.VMEM((1, QCOLS), F32),
+        pltpu.VMEM((1, KCOLS), F32),
+        pltpu.SMEM((256,), jnp.int32),
         pltpu.VMEM((TOKENS, QCOLS), BF16),
         pltpu.VMEM((TOKENS, QCOLS), BF16),
         pltpu.VMEM((TOKENS, QCOLS), F32),
@@ -576,7 +588,7 @@
         gain,
         pltpu.VMEM((4, GAIN_ROWS, 128), F32),
         pltpu.VMEM((8, GAIN_ROWS, 128), F32),
-        sems((3 + QUERY_PIECES,)),
+        sems((6 + QUERY_PIECES,)),
         sems((9,)),
         sems((9,)),
         sems((3,)),
@@ -603,7 +615,7 @@
     held = pl.pallas_call(
         kernel,
         out_shape=[pltpu.VMEM(*shape) for shape in shapes],
-        in_specs=[hbm] * 4 + [vmem] * 2 + [smem],
+        in_specs=[hbm] * 7,
         out_specs=[vmem] * 6,
         scratch_shapes=scratch,
         compiler_params=pltpu.CompilerParams(

time: 48.5 us -> 47.9 us (0.988)
  Pallas kernels: 47.7 us -> 47.1 us
    pallas_call x1, Pallas kernels: 45.3 us -> 44.7 us  [local(): pl.pallas_call(kernel, out_shape=[pltpu.VMEM(*shape) for shape in shapes]...]
where the time goes in v4:
time: 47.9 us; the launch traced here: 47.8 us
  Pallas kernels  47.1 us (98%)
  between operations  0.64 us (1%)
    pallas_call x1, Pallas kernels, local(): pl.pallas_call(kernel, out_shape=[pltpu.VMEM(*shape) for shape in shapes]...  44.7 us
    pallas_call x1, Pallas kernels, local(): pl.pallas_call(write, out_shape=[jax.ShapeDtypeStruct(*shape) for shape i...  2.39 us

profile of v4, /device:TPU:4, one launch (start us, length us, event | category | flops | bytes accessed | tf_op | source)
XLA Modules:
  0.0 47.8 jit_solution(248604341885539904)
XLA Ops:
  0.6 44.7 %shard_map.118 = (bf16[1024,1024]{1,0:T(8,128)(2,1)S(1)}, bf16[1024,1024]{1,0:T(8,128)(2,1)S(1)}, bf16[1024,256]{1,0:T(8,128)(2,1)S(1)}, bf16[1024,256]{1,0:T(8,...) custom-call(bf16[1024,1024]{1,0:T(8,128)(2,1)} %q_in.1, bf16[1024,256]{1,0:T(8,128)(2,1)} %k_in.1, ...), custom_call_target="tpu_custom_call" | custom-call | flops 8000000000 | bytes 10000000 | tf_op jit(solution)/shard_map/pallas_call | solution.py:615
  45.4 2.4 %shard_map.119 = (bf16[1024,1024]{1,0:T(8,128)(2,1)}, bf16[1024,1024]{1,0:T(8,128)(2,1)}, bf16[1024,256]{1,0:T(8,128)(2,1)}, bf16[1024,256]{1,0:T(8,128)(2,1)}, f32[1,1024]{1,0:T(1,128)}, /*index=5*/f32[1,256]{1,0:T(1,128)}) custom-call(bf16[1024,1024]{1,0:T(8,128)(2,1)S(1)} %get-tuple-element.18.refs_0_, bf16[1024,1024]{1,0:T(8,128)(2,1)S(1)} %get-tuple-element.19.refs_1_, ...), custom_call_target="tpu_custom_call" | custom-call | tf_op jit(solution)/shard_map/pallas_call | solution.py:631

commit v5 on v4

--- a/solution.py
+++ b/solution.py
@@ -444,12 +444,6 @@
         copy.start()
     kin_all[head] = kin[...]
 
-    for copy in hin_copies:
-        copy.wait_recv()
-    hin_sum[...] = hin_all[0] + hin_all[1] + hin_all[2] + hin_all[3]
-    hin_back = remote(hin_sum, hin_got, hin_send.at[3], hin_recv.at[3], ctx=prv)
-    hin_back.start()
-
     last_k, last_v = back_copies(HALO_BLOCKS - 1)
     last_k.start()
     for copy in x_copies:
@@ -463,6 +457,11 @@
     ]
     for copy in zy_copies:
         copy.start()
+    for copy in hin_copies:
+        copy.wait_recv()
+    hin_sum[...] = hin_all[0] + hin_all[1] + hin_all[2] + hin_all[3]
+    hin_back = remote(hin_sum, hin_got, hin_send.at[3], hin_recv.at[3], ctx=prv)
+    hin_back.start()
     last_v.start()
 
     def finish_later(s, _):

time: 47.9 us -> 47 us (0.981)
  Pallas kernels: 47.1 us -> 45.8 us
    pallas_call x1, Pallas kernels: 44.7 us -> 43.4 us  [local(): pl.pallas_call(kernel, out_shape=[pltpu.VMEM(*shape) for shape in shapes]...]
where the time goes in v5:
time: 47 us; the launch traced here: 46.4 us
  Pallas kernels  45.8 us (97%)
  between operations  0.64 us (1%)
    pallas_call x1, Pallas kernels, local(): pl.pallas_call(kernel, out_shape=[pltpu.VMEM(*shape) for shape in shapes]...  43.4 us
    pallas_call x1, Pallas kernels, local(): pl.pallas_call(write, out_shape=[jax.ShapeDtypeStruct(*shape) for shape i...  2.39 us

profile of v5, /device:TPU:4, one launch (start us, length us, event | category | flops | bytes accessed | tf_op | source)
XLA Modules:
  0.0 46.4 jit_solution(4355105273370484067)
XLA Ops:
  0.6 43.4 %shard_map.118 = (bf16[1024,1024]{1,0:T(8,128)(2,1)S(1)}, bf16[1024,1024]{1,0:T(8,128)(2,1)S(1)}, bf16[1024,256]{1,0:T(8,128)(2,1)S(1)}, bf16[1024,256]{1,0:T(8,...) custom-call(bf16[1024,1024]{1,0:T(8,128)(2,1)} %q_in.1, bf16[1024,256]{1,0:T(8,128)(2,1)} %k_in.1, ...), custom_call_target="tpu_custom_call" | custom-call | flops 8000000000 | bytes 10000000 | tf_op jit(solution)/shard_map/pallas_call | solution.py:614
  44.0 2.4 %shard_map.119 = (bf16[1024,1024]{1,0:T(8,128)(2,1)}, bf16[1024,1024]{1,0:T(8,128)(2,1)}, bf16[1024,256]{1,0:T(8,128)(2,1)}, bf16[1024,256]{1,0:T(8,128)(2,1)}, f32[1,1024]{1,0:T(1,128)}, /*index=5*/f32[1,256]{1,0:T(1,128)}) custom-call(bf16[1024,1024]{1,0:T(8,128)(2,1)S(1)} %get-tuple-element.18.refs_0_, bf16[1024,1024]{1,0:T(8,128)(2,1)S(1)} %get-tuple-element.19.refs_1_, ...), custom_call_target="tpu_custom_call" | custom-call | tf_op jit(solution)/shard_map/pallas_call | solution.py:630

commit v6 on v5

--- a/solution.py
+++ b/solution.py
@@ -414,6 +414,23 @@
         take_halo(n)
     lax.fori_loop(4, BLOCKS_HERE, late, 0)
 
+    def x_phase(part):
+        rows = pl.ds(part * HEADS, HEADS)
+        return [
+            remote(
+                gains.at[rows], gains_x.at[x, rows],
+                gain_send.at[r - 1 + 10 * part], gain_recv.at[r - 1 + 10 * part], ctx=at_x(r),
+            )
+            for r in range(1, 4)
+        ]
+
+    for t in range(HEADS):
+        gains[t : t + 1] = jnp.sum(q_acc[:, cols(t)], axis=0, keepdims=True)
+    x_copies = x_phase(0)
+    for copy in x_copies:
+        copy.start()
+    gains_x[x, 0:HEADS] = gains[0:HEADS]
+
     for b in range(BLOCKS_HERE):
         rows = slice(HALO + b * BLOCK, HALO + (b + 1) * BLOCK)
         scale = k_col[rows]
@@ -425,18 +442,14 @@
             product = onto * gain if product is None else product + onto * gain
         products[b] = product
 
-    for t in range(HEADS):
-        gains[t : t + 1] = jnp.sum(q_acc[:, cols(t)], axis=0, keepdims=True)
     for t in range(GROUPS):
         gains[HEADS + t : HEADS + t + 1] = jnp.sum(k_acc[:, cols(t)], axis=0, keepdims=True)
     gains[HEADS + GROUPS :] = jnp.zeros((GAIN_ROWS - HEADS - GROUPS, 128), F32)
-    x_copies = [
-        remote(gains, gains_x.at[x], gain_send.at[r - 1], gain_recv.at[r - 1], ctx=at_x(r))
-        for r in range(1, 4)
-    ]
-    for copy in x_copies:
-        copy.start()
-    gains_x[x] = gains[...]
+    key_copies = x_phase(1)
+    for copy in key_copies:
+        copy.start()
+    gains_x[x, HEADS:] = gains[HEADS:]
+    x_copies = x_copies + key_copies
     for b in range(BLOCKS_HERE):
         kin[b : b + 1] = row_sums(products[b])
     kin_copies = exchange(kin, kin_all, kin_send, kin_recv)
@@ -600,8 +613,8 @@
         sems((3,)),
         sems((4,)),
         sems((4,)),
-        sems((10,)),
-        sems((10,)),
+        sems((13,)),
+        sems((13,)),
     ]
     shapes = [
         ((TOKENS, QCOLS), BF16),

time: 47 us -> 47 us (level)
  no operation moved by 1% of the time
where the time goes in v6:
time: 47 us; the launch traced here: 46.4 us
  Pallas kernels  45.8 us (97%)
  between operations  0.64 us (1%)
    pallas_call x1, Pallas kernels, local(): pl.pallas_call(kernel, out_shape=[pltpu.VMEM(*shape) for shape in shapes]...  43.4 us
    pallas_call x1, Pallas kernels, local(): pl.pallas_call(write, out_shape=[jax.ShapeDtypeStruct(*shape) for shape i...  2.39 us

profile of v6, /device:TPU:4, one launch (start us, length us, event | category | flops | bytes accessed | tf_op | source)
XLA Modules:
  0.0 46.4 jit_solution(13503629708014654482)
XLA Ops:
  0.6 43.4 %shard_map.118 = (bf16[1024,1024]{1,0:T(8,128)(2,1)S(1)}, bf16[1024,1024]{1,0:T(8,128)(2,1)S(1)}, bf16[1024,256]{1,0:T(8,128)(2,1)S(1)}, bf16[1024,256]{1,0:T(8,...) custom-call(bf16[1024,1024]{1,0:T(8,128)(2,1)} %q_in.1, bf16[1024,256]{1,0:T(8,128)(2,1)} %k_in.1, ...), custom_call_target="tpu_custom_call" | custom-call | flops 8000000000 | bytes 10000000 | tf_op jit(solution)/shard_map/pallas_call | solution.py:627
  44.0 2.4 %shard_map.119 = (bf16[1024,1024]{1,0:T(8,128)(2,1)}, bf16[1024,1024]{1,0:T(8,128)(2,1)}, bf16[1024,256]{1,0:T(8,128)(2,1)}, bf16[1024,256]{1,0:T(8,128)(2,1)}, f32[1,1024]{1,0:T(1,128)}, /*index=5*/f32[1,256]{1,0:T(1,128)}) custom-call(bf16[1024,1024]{1,0:T(8,128)(2,1)S(1)} %get-tuple-element.18.refs_0_, bf16[1024,1024]{1,0:T(8,128)(2,1)S(1)} %get-tuple-element.19.refs_1_, ...), custom_call_target="tpu_custom_call" | custom-call | tf_op jit(solution)/shard_map/pallas_call | solution.py:643
